TPU v7x, 256 devices: a whole 4x4x8 slice. The times are simulated.
256 devices in a mesh: groups: 64 (over z, y, core), rays: 4 (over x).
Axes of the slice: x: 4, y: 4, z: 8, core: 2. Of those that a mesh axis runs over, the one named last changes fastest.
Arguments:
- excitation: bfloat16 [3, 64, 32768], P(None, None, ('groups', 'rays')), may hold values from -6 to 6
- cycle: bfloat16 [8, 64, 32768], P(None, None, ('groups', 'rays')), may hold values from -6 to 6
- near_blocks: bfloat16 [64, 5, 8, 512, 512], P('groups', None, None, 'rays'), may hold values from -0.0390625 to 0.0390625
- near_list: int32 [64, 5], P('groups'), may hold values from 0 to 4, as said below
- near_count: int32 [64], P('groups'), may hold values from 1 to 5, as said below
- newest: int32 [8], replicated, may hold values from 0 to 7, each once
- inverse: bfloat16 [512, 32768], P(None, ('groups', 'rays')), may hold values from -0.25 to 0.25
- radiate: bfloat16 [1024, 32768], P(None, ('groups', 'rays')), may hold values from -0.25 to 0.25
- translate: float32 [64, 64, 1024], P('groups', None, 'rays'), may hold values from -0.75 to 0.75
- receive: bfloat16 [1024, 32768], P('rays', 'groups'), may hold values from -0.1875 to 0.1875
Outputs:
- currents: bfloat16 [3, 64, 32768], P(None, None, ('groups', 'rays'))
Inputs may be any that keep to these rules, and one draw needn't show every extreme that they name: `near_list`: each row holds every number 0 to 4 once; its first near_count entries name the near groups, always include 2 (the group itself) and never a group outside the range. `near_count`: some group lists all 5 entries. `newest`: holds each slot once.
All inputs are finite; a program needn't handle non-finite values.
Results may differ from a plain program's by a relative error of at most 0.018.
Values may be sent and summed in bfloat16 or wider, within the bound.
A program may use at most 64 MiB of HBM per device.

v0:
```python
import jax
import jax.numpy as jnp
from jax import lax
from jax.sharding import PartitionSpec as P

REACH = 2
STEPS = 3


def shifted(block, axis, distance):
    devices = range(lax.axis_size(axis))
    route = [(i - distance, i) for i in devices if i - distance in devices]
    return lax.ppermute(block, axis, route)


def local(
    excitation,
    cycle,
    near_blocks,
    near_list,
    near_count,
    newest,
    inverse,
    radiate,
    translate,
    receive,
):
    group_index = lax.axis_index("groups")
    group_total = lax.axis_size("groups")
    ray_index = lax.axis_index("rays")
    slot_total = cycle.shape[0]
    waves = cycle.shape[1]
    width = cycle.shape[2]
    group_size = near_blocks.shape[4]
    spread = 2 * REACH + 1
    entries = jnp.arange(near_list.shape[1], dtype=jnp.int32)
    sources = group_index + near_list[0] - REACH
    valid = (entries < near_count[0]) & (sources >= 0) & (sources < group_total)
    every = jnp.arange(group_total, dtype=jnp.int32)
    marked = jnp.any(valid[:, None] & (sources[:, None] == every[None, :]), axis=0)
    weights = translate[0] * jnp.where(marked, 0.0, 1.0).astype(jnp.float32)[:, None]
    choose = (
        valid[:, None] & (near_list[0][:, None] == jnp.arange(spread, dtype=jnp.int32)[None, :])
    ).astype(jnp.bfloat16)
    blocks = near_blocks[0].reshape(-1, group_size)
    pieces_list = []
    for offset in range(-REACH, REACH + 1):
        if offset == 0:
            pieces_list.append(cycle)
        else:
            pieces_list.append(shifted(cycle, "groups", -offset))
    nearby = jnp.stack(pieces_list)

    def fold_far(piece):
        return jnp.einsum(
            "hr,hwr->wr", weights, piece.astype(jnp.float32), precision=lax.Precision.HIGHEST
        )

    def far_only(slab):
        return fold_far(lax.all_gather(slab[None], "groups", axis=0, tiled=True))

    start_slot = newest[0]
    partial_value = lax.dot_general(
        lax.dynamic_index_in_dim(cycle, start_slot, 0, keepdims=False),
        radiate,
        (((1,), (1,)), ((), ())),
        preferred_element_type=jnp.float32,
    )
    field = far_only(
        lax.psum_scatter(partial_value, "rays", scatter_dimension=1, tiled=True).astype(
            jnp.bfloat16
        )
    )
    outputs = []
    for step in range(STEPS):
        slot_now = (start_slot + step) % slot_total
        lag_slots = (slot_now - jnp.arange(slot_total, dtype=jnp.int32)) % slot_total
        picked = jnp.einsum(
            "bo,oswc->bswc", choose, nearby, preferred_element_type=jnp.float32
        ).astype(jnp.bfloat16)
        lagged = jnp.take(picked, lag_slots, axis=1)
        near_rows = lagged.transpose(2, 0, 1, 3).reshape(waves, -1)
        near = jnp.dot(near_rows, blocks, preferred_element_type=jnp.float32)
        far = jnp.dot(field.astype(jnp.bfloat16), receive, preferred_element_type=jnp.float32)
        own = lax.dynamic_update_slice_in_dim(
            jnp.zeros((waves, group_size), jnp.float32),
            excitation[step].astype(jnp.float32),
            ray_index * width,
            1,
        )
        term = own - near - far
        drive = lax.psum(term, "rays").astype(jnp.bfloat16)
        current = jnp.dot(drive, inverse, preferred_element_type=jnp.float32).astype(jnp.bfloat16)
        outputs.append(current)
        write_slot = (slot_now + 1) % slot_total
        if step + 1 < STEPS:
            aggregate_partial_value = lax.dot_general(
                current, radiate, (((1,), (1,)), ((), ())), preferred_element_type=jnp.float32
            )
            slab = lax.psum_scatter(
                aggregate_partial_value, "rays", scatter_dimension=1, tiled=True
            ).astype(jnp.bfloat16)
            field = far_only(slab)
            fresh_list = []
            for offset in range(-REACH, REACH + 1):
                if offset == 0:
                    fresh_list.append(current)
                else:
                    fresh_list.append(shifted(current, "groups", -offset))
            fresh = jnp.stack(fresh_list)
            nearby = lax.dynamic_update_slice_in_dim(nearby, fresh[:, None], write_slot, 1)
    return jnp.stack(outputs)


def solution(mesh):
    placed = (
        P(None, None, ("groups", "rays")),
        P(None, None, ("groups", "rays")),
        P("groups", None, None, "rays", None),
        P("groups", None),
        P("groups"),
        P(),
        P(None, ("groups", "rays")),
        P(None, ("groups", "rays")),
        P("groups", None, "rays"),
        P("rays", "groups"),
    )
    return jax.shard_map(
        local,
        mesh=mesh,
        in_specs=placed,
        out_specs=P(None, None, ("groups", "rays")),
        check_vma=False,
    )
```

profile of v0, /device:TPU:1, one launch (start us, length us, event | category | flops | bytes accessed | tf_op | source)
XLA Modules:
  0.0 384.8 jit_solution(9432682228357418655)
XLA Ops:
  8.5 1.6 fusion.14
  10.2 24.8 %reduce-scatter.4.cloned.1.call-done = f32[64,256]{1,0:T(8,128)} async-done(((f32[64,1024]{1,0:T(8,128)}), f32[64,256]{1,0:T(8,128)}) %reduce-scatter.4.cloned.1.call-update) | async-done | bytes 65552 | tf_op jit(solution)/shard_map/reduce_scatter | solution.py:70
  35.0 1.5 convert_element_type.73
  36.6 3.1 collective-permute-start
  39.7 6.1 %collective-permute-start.1 = (bf16[8,64,128]{2,1,0:T(8,128)(2,1)}, bf16[8,64,128]{2,1,0:T(8,128)(2,1)S(1)}, u32[]{:S(2)}, u32[]{:S(2)}) collective-permute-start(bf16[8,64,128]{2,1,0:T(8,128)(2,1)} %param.13), channel_id=1, source_target_pairs={{0,4},{4,8},{8,12},{12,16},{16,20},{20,24},{24,28},{28,32},{32,36}... | collective-permute-start | bytes 393224 | tf_op jit(solution)/shard_map/ppermute | solution.py:13
  45.9 1.9 collective-permute-start.2
  52.6 1.6 fusion.7
  56.2 2.1 stack.67
  60.6 3.6 convolution_subtract_fusion.5
  64.2 53.7 %all-gather.7.cloned.1.call-done = bf16[4096,256]{1,0:T(8,128)(2,1)} async-done(((bf16[64,256]{1,0:T(8,128)(2,1)}), bf16[4096,256]{1,0:T(8,128)(2,1)}) %all-gather.7.cloned.1.call-update) | async-done | bytes 2097168 | tf_op jit(solution)/shard_map/all_gather | solution.py:60
  118.0 2.1 multiply_reduce_fusion.2
  120.3 14.6 %all-reduce.3 = bf16[64,512]{1,0:T(8,128)(2,1)S(1)} all-reduce(f32[64,512]{1,0:T(8,128)S(1)} %convolution_subtract_fusion.4), channel_id=1, replica_groups=mesh['groups'=64,'rays'=4] {'rays'}, use_global_device_ids=true, to_apply=%region_2.4 | all-reduce | flops 32768 | bytes 196608 | tf_op jit(solution)/shard_map/psum | solution.py:92
  136.0 20.5 %reduce-scatter.6.cloned.1.call-done = f32[64,256]{1,0:T(8,128)} async-done(((f32[64,1024]{1,0:T(8,128)}), f32[64,256]{1,0:T(8,128)}) %reduce-scatter.6.cloned.1.call-update) | async-done | bytes 65552 | tf_op jit(solution)/shard_map/reduce_scatter | solution.py:100
  156.5 1.5 convert_element_type.80
  161.2 3.1 collective-permute-start.4
  164.3 6.2 %collective-permute-start.5 = (bf16[64,128]{1,0:T(8,128)(2,1)S(1)}, bf16[64,128]{1,0:T(8,128)(2,1)S(1)}, u32[]{:S(2)}, u32[]{:S(2)}) collective-permute-start(bf16[64,128]{1,0:T(8,128)(2,1)S(1)} %convolution_convert_fusion.5), channel_id=1, source_target_pairs={{0,4},{4,8},{8,12},{12,16},{16,20},{20,24},{24,28},{28,32},{32,36}... | collective-permute-start | bytes 49160 | tf_op jit(solution)/shard_map/ppermute | solution.py:13
  170.5 1.9 collective-permute-start.6
  175.6 1.8 collective-permute-done.7
  180.8 3.6 convolution_subtract_fusion.3
  184.4 54.5 %all-gather.9.cloned.1.call-done = bf16[4096,256]{1,0:T(8,128)(2,1)} async-done(((bf16[64,256]{1,0:T(8,128)(2,1)}), bf16[4096,256]{1,0:T(8,128)(2,1)}) %all-gather.9.cloned.1.call-update) | async-done | bytes 2097168 | tf_op jit(solution)/shard_map/all_gather | solution.py:60
  238.9 2.1 multiply_reduce_fusion.1
  241.3 14.6 %all-reduce.4 = bf16[64,512]{1,0:T(8,128)(2,1)S(1)} all-reduce(f32[64,512]{1,0:T(8,128)S(1)} %convolution_subtract_fusion.2), channel_id=1, replica_groups=mesh['groups'=64,'rays'=4] {'rays'}, use_global_device_ids=true, to_apply=%region_4.6 | all-reduce | flops 32768 | bytes 196608 | tf_op jit(solution)/shard_map/psum | solution.py:92
  257.0 20.5 %reduce-scatter.8.cloned.1.call-done = f32[64,256]{1,0:T(8,128)} async-done(((f32[64,1024]{1,0:T(8,128)}), f32[64,256]{1,0:T(8,128)}) %reduce-scatter.8.cloned.1.call-update) | async-done | bytes 65552 | tf_op jit(solution)/shard_map/reduce_scatter | solution.py:100
  279.7 3.1 collective-permute-start.8
  282.8 6.2 %collective-permute-start.9 = (bf16[64,128]{1,0:T(8,128)(2,1)S(1)}, bf16[64,128]{1,0:T(8,128)(2,1)S(1)}, u32[]{:S(2)}, u32[]{:S(2)}) collective-permute-start(bf16[64,128]{1,0:T(8,128)(2,1)S(1)} %convolution_convert_fusion.4), channel_id=1, source_target_pairs={{0,4},{4,8},{8,12},{12,16},{16,20},{20,24},{24,28},{28,32},{32,36}... | collective-permute-start | bytes 49160 | tf_op jit(solution)/shard_map/ppermute | solution.py:13
  289.0 1.9 collective-permute-start.10
  290.9 1.5 collective-permute-start.11
  292.6 1.5 collective-permute-done.10
  298.0 3.5 convolution_subtract_fusion.1
  301.5 58.7 %all-gather.11.cloned.1.call-done = bf16[4096,256]{1,0:T(8,128)(2,1)} async-done(((bf16[64,256]{1,0:T(8,128)(2,1)}), bf16[4096,256]{1,0:T(8,128)(2,1)}) %all-gather.11.cloned.1.call-update) | async-done | bytes 2097168 | tf_op jit(solution)/shard_map/all_gather | solution.py:60
  360.2 2.0 multiply_reduce_fusion
  362.6 14.6 %all-reduce.5 = bf16[64,512]{1,0:T(8,128)(2,1)S(1)} all-reduce(f32[64,512]{1,0:T(8,128)S(1)} %convolution_subtract_fusion), channel_id=1, replica_groups=mesh['groups'=64,'rays'=4] {'rays'}, use_global_device_ids=true, to_apply=%region_6.8 | all-reduce | flops 32768 | bytes 196608 | tf_op jit(solution)/shard_map/psum | solution.py:92
  (116 shorter events, 26.8 us)
Async XLA Ops:
  6.5 51.8 %copy-start.7 = (s32[1,5]{1,0:T(1,128)S(1)}, s32[1,5]{1,0:T(1,128)}, u32[]{:S(2)}) copy-start(s32[1,5]{1,0:T(1,128)} %param.15) | copy-start | bytes 64
  6.5 28.5 %reduce-scatter.4.cloned.1.call-start = ((), (), s32[]{:S(2)}) async-start(), calls=%async_computation.3 | async-start | bytes 327680 | tf_op jit(solution)/shard_map/reduce_scatter | solution.py:70
  10.2 107.8 %all-gather.7.cloned.1.call-start = ((), (), s32[]{:S(2)}) async-start(), calls=%async_computation.6 | async-start | bytes 2129920 | tf_op jit(solution)/shard_map/all_gather | solution.py:60
  36.5 120.0 %reduce-scatter.6.cloned.1.call-start = ((), (), s32[]{:S(2)}) async-start(), calls=%async_computation.4 | async-start | bytes 327680 | tf_op jit(solution)/shard_map/reduce_scatter | solution.py:100
  36.6 18.8 %collective-permute-start = (bf16[8,64,128]{2,1,0:T(8,128)(2,1)}, bf16[8,64,128]{2,1,0:T(8,128)(2,1)S(1)}, u32[]{:S(2)}, u32[]{:S(2)}) collective-permute-start(bf16[8,64,128]{2,1,0:T(8,128)(2,1)} %param.13), channel_id=1, source_target_pairs={{0,8},{4,12},{8,16},{12,20},{16,24},{20,28},{24,32},{28,36},{32,40... | collective-permute-start | bytes 393224 | tf_op jit(solution)/shard_map/ppermute | solution.py:13
  39.7 15.8 %collective-permute-start.1 = (bf16[8,64,128]{2,1,0:T(8,128)(2,1)}, bf16[8,64,128]{2,1,0:T(8,128)(2,1)S(1)}, u32[]{:S(2)}, u32[]{:S(2)}) collective-permute-start(bf16[8,64,128]{2,1,0:T(8,128)(2,1)} %param.13), channel_id=1, source_target_pairs={{0,4},{4,8},{8,12},{12,16},{16,20},{20,24},{24,28},{28,32},{32,36}... | collective-permute-start | bytes 393224 | tf_op jit(solution)/shard_map/ppermute | solution.py:13
  45.9 9.9 %collective-permute-start.2 = (bf16[8,64,128]{2,1,0:T(8,128)(2,1)}, bf16[8,64,128]{2,1,0:T(8,128)(2,1)S(1)}, u32[]{:S(2)}, u32[]{:S(2)}) collective-permute-start(bf16[8,64,128]{2,1,0:T(8,128)(2,1)} %param.13), channel_id=1, source_target_pairs={{4,0},{8,4},{12,8},{16,12},{20,16},{24,20},{28,24},{32,28},{36,32}... | collective-permute-start | bytes 393224 | tf_op jit(solution)/shard_map/ppermute | solution.py:13
  47.8 8.2 %collective-permute-start.3 = (bf16[8,64,128]{2,1,0:T(8,128)(2,1)}, bf16[8,64,128]{2,1,0:T(8,128)(2,1)S(1)}, u32[]{:S(2)}, u32[]{:S(2)}) collective-permute-start(bf16[8,64,128]{2,1,0:T(8,128)(2,1)} %param.13), channel_id=1, source_target_pairs={{8,0},{12,4},{16,8},{20,12},{24,16},{28,20},{32,24},{36,28},{40,32... | collective-permute-start | bytes 393224 | tf_op jit(solution)/shard_map/ppermute | solution.py:13
  51.7 8.1 %copy-start.10 = (pred[5]{0:T(512)(128)(4,1)}, pred[5]{0:T(512)(128)(4,1)S(1)}, u32[]{:S(2)}) copy-start(pred[5]{0:T(512)(128)(4,1)S(1)} %get-tuple-element.6) | copy-start | bytes 19
  59.8 58.1 %copy-start.4 = (f32[256,64]{0,1:T(8,128)S(1)}, f32[256,64]{0,1:T(8,128)}, u32[]{:S(2)}) copy-start(f32[256,64]{0,1:T(8,128)} %fusion.7) | copy-start | bytes 196612
  60.6 59.5 %copy-start.1 = (bf16[256,512]{1,0:T(8,128)(2,1)S(1)}, bf16[256,512]{1,0:T(8,128)(2,1)}, u32[]{:S(2)}) copy-start(bf16[256,512]{1,0:T(8,128)(2,1)} %param.21) | copy-start | bytes 786436
  60.6 74.3 %copy-start.3 = (bf16[512,128]{1,0:T(8,128)(2,1)S(1)}, bf16[512,128]{1,0:T(8,128)(2,1)}, u32[]{:S(2)}) copy-start(bf16[512,128]{1,0:T(8,128)(2,1)} %param.18) | copy-start | bytes 393220
  60.6 97.4 %copy-start.15 = (s32[8]{0:T(128)S(1)}, s32[8]{0:T(128)}, u32[]{:S(2)}) copy-start(s32[8]{0:T(128)} %param.17) | copy-start | bytes 100
  64.2 113.5 %copy-start.8 = (s32[1,5]{1,0:T(1,128)S(1)}, s32[1,5]{1,0:T(1,128)}, u32[]{:S(2)}) copy-start(s32[1,5]{1,0:T(1,128)} %param.15) | copy-start | bytes 64
  64.2 113.5 %copy-start.11 = (pred[5]{0:T(512)(128)(4,1)S(1)}, pred[5]{0:T(512)(128)(4,1)}, u32[]{:S(2)}) copy-start(pred[5]{0:T(512)(128)(4,1)} %copy-done.10) | copy-start | bytes 19
  136.0 102.9 %all-gather.9.cloned.1.call-start = ((), (), s32[]{:S(2)}) async-start(), calls=%async_computation.7 | async-start | bytes 2129920 | tf_op jit(solution)/shard_map/all_gather | solution.py:60
  158.0 119.5 %reduce-scatter.8.cloned.1.call-start = ((), (), s32[]{:S(2)}) async-start(), calls=%async_computation.5 | async-start | bytes 327680 | tf_op jit(solution)/shard_map/reduce_scatter | solution.py:100
  161.2 13.2 %collective-permute-start.4 = (bf16[64,128]{1,0:T(8,128)(2,1)S(1)}, bf16[64,128]{1,0:T(8,128)(2,1)S(1)}, u32[]{:S(2)}, u32[]{:S(2)}) collective-permute-start(bf16[64,128]{1,0:T(8,128)(2,1)S(1)} %convolution_convert_fusion.5), channel_id=1, source_target_pairs={{0,8},{4,12},{8,16},{12,20},{16,24},{20,28},{24,32},{28,36},{32,40... | collective-permute-start | bytes 49160 | tf_op jit(solution)/shard_map/ppermute | solution.py:13
  164.3 10.1 %collective-permute-start.5 = (bf16[64,128]{1,0:T(8,128)(2,1)S(1)}, bf16[64,128]{1,0:T(8,128)(2,1)S(1)}, u32[]{:S(2)}, u32[]{:S(2)}) collective-permute-start(bf16[64,128]{1,0:T(8,128)(2,1)S(1)} %convolution_convert_fusion.5), channel_id=1, source_target_pairs={{0,4},{4,8},{8,12},{12,16},{16,20},{20,24},{24,28},{28,32},{32,36}... | collective-permute-start | bytes 49160 | tf_op jit(solution)/shard_map/ppermute | solution.py:13
  170.5 5.1 %collective-permute-start.6 = (bf16[64,128]{1,0:T(8,128)(2,1)S(1)}, bf16[64,128]{1,0:T(8,128)(2,1)S(1)}, u32[]{:S(2)}, u32[]{:S(2)}) collective-permute-start(bf16[64,128]{1,0:T(8,128)(2,1)S(1)} %convolution_convert_fusion.5), channel_id=1, source_target_pairs={{4,0},{8,4},{12,8},{16,12},{20,16},{24,20},{28,24},{32,28},{36,32}... | collective-permute-start | bytes 49160 | tf_op jit(solution)/shard_map/ppermute | solution.py:13
  172.5 4.9 %collective-permute-start.7 = (bf16[64,128]{1,0:T(8,128)(2,1)S(1)}, bf16[64,128]{1,0:T(8,128)(2,1)S(1)}, u32[]{:S(2)}, u32[]{:S(2)}) collective-permute-start(bf16[64,128]{1,0:T(8,128)(2,1)S(1)} %convolution_convert_fusion.5), channel_id=1, source_target_pairs={{8,0},{12,4},{16,8},{20,12},{24,16},{28,20},{32,24},{36,28},{40,32... | collective-permute-start | bytes 49160 | tf_op jit(solution)/shard_map/ppermute | solution.py:13
  180.0 58.9 %copy-start.5 = (f32[256,64]{0,1:T(8,128)S(1)}, f32[256,64]{0,1:T(8,128)}, u32[]{:S(2)}) copy-start(f32[256,64]{0,1:T(8,128)} %fusion.7) | copy-start | bytes 196612
  180.8 60.3 %copy-start.2 = (bf16[256,512]{1,0:T(8,128)(2,1)S(1)}, bf16[256,512]{1,0:T(8,128)(2,1)}, u32[]{:S(2)}) copy-start(bf16[256,512]{1,0:T(8,128)(2,1)} %param.21) | copy-start | bytes 786436
  180.8 111.6 %copy-start.14 = (s32[8]{0:T(128)S(1)}, s32[8]{0:T(128)}, u32[]{:S(2)}) copy-start(s32[8]{0:T(128)} %get-tuple-element.8) | copy-start | bytes 100
  180.8 115.0 %copy-start.9 = (s32[1,5]{1,0:T(1,128)S(1)}, s32[1,5]{1,0:T(1,128)}, u32[]{:S(2)}) copy-start(s32[1,5]{1,0:T(1,128)} %param.15) | copy-start | bytes 64
  180.8 115.0 %copy-start.12 = (pred[5]{0:T(512)(128)(4,1)S(1)}, pred[5]{0:T(512)(128)(4,1)}, u32[]{:S(2)}) copy-start(pred[5]{0:T(512)(128)(4,1)} %copy-done.10) | copy-start | bytes 19
  238.9 58.1 %copy-start.13 = (pred[8]{0:T(512)(128)(4,1)S(1)}, pred[8]{0:T(512)(128)(4,1)}, u32[]{:S(2)}) copy-start(pred[8]{0:T(512)(128)(4,1)} %get-tuple-element.10) | copy-start | bytes 28
  256.9 103.3 %all-gather.11.cloned.1.call-start = ((), (), s32[]{:S(2)}) async-start(), calls=%async_computation.8 | async-start | bytes 2129920 | tf_op jit(solution)/shard_map/all_gather | solution.py:60
  279.7 12.8 %collective-permute-start.8 = (bf16[64,128]{1,0:T(8,128)(2,1)S(1)}, bf16[64,128]{1,0:T(8,128)(2,1)S(1)}, u32[]{:S(2)}, u32[]{:S(2)}) collective-permute-start(bf16[64,128]{1,0:T(8,128)(2,1)S(1)} %convolution_convert_fusion.4), channel_id=1, source_target_pairs={{0,8},{4,12},{8,16},{12,20},{16,24},{20,28},{24,32},{28,36},{32,40... | collective-permute-start | bytes 49160 | tf_op jit(solution)/shard_map/ppermute | solution.py:13
  282.8 9.7 %collective-permute-start.9 = (bf16[64,128]{1,0:T(8,128)(2,1)S(1)}, bf16[64,128]{1,0:T(8,128)(2,1)S(1)}, u32[]{:S(2)}, u32[]{:S(2)}) collective-permute-start(bf16[64,128]{1,0:T(8,128)(2,1)S(1)} %convolution_convert_fusion.4), channel_id=1, source_target_pairs={{0,4},{4,8},{8,12},{12,16},{16,20},{20,24},{24,28},{28,32},{32,36}... | collective-permute-start | bytes 49160 | tf_op jit(solution)/shard_map/ppermute | solution.py:13
  289.0 5.1 %collective-permute-start.10 = (bf16[64,128]{1,0:T(8,128)(2,1)S(1)}, bf16[64,128]{1,0:T(8,128)(2,1)S(1)}, u32[]{:S(2)}, u32[]{:S(2)}) collective-permute-start(bf16[64,128]{1,0:T(8,128)(2,1)S(1)} %convolution_convert_fusion.4), channel_id=1, source_target_pairs={{4,0},{8,4},{12,8},{16,12},{20,16},{24,20},{28,24},{32,28},{36,32}... | collective-permute-start | bytes 49160 | tf_op jit(solution)/shard_map/ppermute | solution.py:13
  290.9 4.5 %collective-permute-start.11 = (bf16[64,128]{1,0:T(8,128)(2,1)S(1)}, bf16[64,128]{1,0:T(8,128)(2,1)S(1)}, u32[]{:S(2)}, u32[]{:S(2)}) collective-permute-start(bf16[64,128]{1,0:T(8,128)(2,1)S(1)} %convolution_convert_fusion.4), channel_id=1, source_target_pairs={{8,0},{12,4},{16,8},{20,12},{24,16},{28,20},{32,24},{36,28},{40,32... | collective-permute-start | bytes 49160 | tf_op jit(solution)/shard_map/ppermute | solution.py:13
  (2 other events, 5.4 us)
Sparse Core Ops, SparseCore 0:
  10.3 24.6 reduce-scatter.3
  38.2 79.7 all-gather.6
  136.1 20.3 reduce-scatter.5
  159.1 79.7 all-gather.8
  257.1 20.3 reduce-scatter.7
  280.5 79.6 all-gather.10
where the time goes:
time: 387 us; the launch traced here: 385 us
  waiting for transfers between devices  238 us (61%)
  blocking collectives  43.7 us (11%)
  starting transfers between devices  37.9 us (10%)
  other arithmetic  19.3 us (5%)
  between operations  18.2 us (5%)
  matrix products  16.6 us (4%)
  local copies, waits for them, and re-layouts  10.6 us (3%)
    all_gather x3, waiting for transfers between devices, far_only(): return fold_far(lax.all_gather(slab[None], 'groups', axis=0, tiled=True))  167 us
    psum x3, blocking collectives, local(): drive = lax.psum(term, 'rays').astype(jnp.bfloat16)  43.7 us
    reduce_scatter x2, waiting for transfers between devices, local(): lax.psum_scatter(aggregate_partial_value, 'rays', scatter_dimension=1, ti...  40.9 us
    ppermute x12, starting transfers between devices, shifted(): return lax.ppermute(block, axis, route)  37.7 us
    reduce_scatter x1, waiting for transfers between devices, local(): lax.psum_scatter(partial_value, 'rays', scatter_dimension=1, tiled=True)  24.8 us
    dot_general x3, matrix products, local(): near = jnp.dot(near_rows, blocks, preferred_element_type=jnp.float32)  10.6 us
  transfers between devices with their start and end apart: 18, of which 10 were waited for; matrix products, arithmetic and copies ran while one was open for 8% of the time, Pallas kernels for 0%

commit v1 on v0

v1 whole, which is shorter than its diff:
```python
import functools

import jax
import jax.numpy as jnp
from jax import lax
from jax.experimental import pallas as pl
from jax.experimental.pallas import tpu as pltpu
from jax.sharding import PartitionSpec as P

REACH = 2
NEAR_SHIFTS = (-2, -1, 1, 2)
MESH = pl.DeviceIdType.MESH
F32 = jnp.float32
BF16 = jnp.bfloat16


def kernel(
    n,
    inner,
    copies_of_fold,
    m,
    exc_hbm,
    cyc_hbm,
    blocks_hbm,
    list_hbm,
    count_hbm,
    newest_hbm,
    inv_hbm,
    rad_hbm,
    tr_hbm,
    rec_hbm,
    out_ref,
    list_ref,
    count_ref,
    newest_ref,
    exc,
    cyc,
    blocks,
    tr,
    rad,
    inv,
    rs_send,
    rs_recv,
    rad_full,
    inv_full,
    slab_of_drive,
    rec_full,
    nearby,
    fresh_first,
    fresh_second,
    w_send,
    w_recv,
    w_both,
    turn_s,
    turn_f,
    s_send,
    s_recv,
    f_send,
    f_recv,
    base,
    p_send,
    p_recv,
    own,
    row_sem,
    load_sems,
    x_send,
    x_recv,
    w_sems,
    s_sems,
    f_sems,
    near_send,
    near_recv,
    p_sems,
):
    steps, waves, width = exc.shape
    slots = cyc.shape[0]
    entries = list_ref.shape[1]
    size = m * width
    rays = tr.shape[1]
    outer = n // inner
    chunks = n // copies_of_fold
    rows = rays // (2 * chunks)
    g = lax.axis_index("groups")
    r = lax.axis_index("rays")
    go = g // inner
    gi = g - go * inner
    pair = go // 2
    plane = go - 2 * pair
    chunk = plane * inner + gi
    first_target = g - chunk
    mine = pl.ds(pl.multiple_of(r * width, width), width)
    dims = (((1,), (1,)), ((), ()))
    fresh_of = (fresh_first, fresh_second)
    ray_order = sorted(range(1, m), key=lambda d: -min(d, m - d))
    inner_order = sorted(range(inner), key=lambda d: -min(d, inner - d))

    def wrap(x, limit):
        return jnp.where(x >= limit, x - limit, x)

    inner_place = [wrap(gi + d, inner) for d in range(inner)]
    ray_place = [wrap(r + d, m) for d in range(m)]

    def near_group(d):
        return wrap(g + d + n, n) if d < 0 else wrap(g + d, n)

    def other_ray(d):
        return ray_place[d]

    def remote(src, dst, send_sem, recv_sem, group, ray):
        return pltpu.make_async_remote_copy(
            src_ref=src,
            dst_ref=dst,
            send_sem=send_sem,
            recv_sem=recv_sem,
            device_id=(group, ray),
            device_id_type=MESH,
        )

    def each_peer(act):
        def body(k, carry):
            shift, change = carry
            place = wrap(go + shift, outer)
            other = place * inner
            bit = place - 2 * (place // 2)
            for d in inner_order:
                act(other + inner_place[d], bit * inner + inner_place[d])
            return shift + change, jnp.where(change < 0, 1 - change, -1 - change)

        lax.fori_loop(0, outer - 1, body, (jnp.int32(outer // 2), jnp.int32(-1)))
        for d in inner_order:
            if d:
                act(go * inner + inner_place[d], plane * inner + inner_place[d])

    def each_target(act, with_self):
        for d in inner_order:
            act((1 - plane) * inner + inner_place[d])
        for d in inner_order:
            if d or with_self:
                act(plane * inner + inner_place[d])

    def wait_blocks(like, sem, count=None):
        part = like.at[pl.ds(0, like.shape[0] - 1 if count is None else count)]
        pltpu.make_async_copy(part, part, sem).wait()

    def near_copies(src, dst, index):
        return [
            remote(
                src,
                dst.at[REACH - shift],
                near_send.at[index, k],
                near_recv.at[index, k],
                near_group(shift),
                r,
            )
            for k, shift in enumerate(NEAR_SHIFTS)
        ]

    def ray_copies(src_of, dst, index):
        return [
            remote(
                src_of(d), dst, x_send.at[index, d - 1], x_recv.at[index, d - 1], g, other_ray(d)
            )
            for d in ray_order
        ]

    barrier = pltpu.get_barrier_semaphore()
    greeted = [(g, other_ray(d)) for d in ray_order]
    greeted += [(go * inner + inner_place[d], r) for d in inner_order if d]
    row_peers = [(wrap(go + d, outer) * inner + gi, r) for d in range(1, outer)]
    greeted += row_peers
    greeted += [(near_group(d), r) for d in NEAR_SHIFTS]
    for device in greeted:
        pl.semaphore_signal(barrier, inc=1, device_id=device, device_id_type=MESH)

    rows_here = pl.ds(pl.multiple_of(r * rays, rays), rays)
    pairs = (
        (newest_hbm, newest_ref),
        (cyc_hbm, cyc),
        (rad_hbm, rad),
        (list_hbm, list_ref),
        (count_hbm, count_ref),
        (tr_hbm.at[0], tr),
        (rad_hbm.at[rows_here, :], rad_full.at[:, mine]),
        (blocks_hbm.at[0], blocks),
        (inv_hbm, inv_full.at[:, mine]),
        (inv_hbm, inv),
        (cyc_hbm, nearby.at[REACH]),
        (rec_hbm, rec_full.at[rows_here, :]),
        (exc_hbm, exc),
    )
    loads = [
        pltpu.make_async_copy(src, dst, load_sems.at[i]) for i, (src, dst) in enumerate(pairs)
    ]
    for load in loads:
        load.start()
    (
        load_newest,
        load_cyc,
        load_all_rad,
        load_list,
        load_count,
        load_tr,
        load_rad,
        load_blocks,
        load_inv,
        load_own_inv,
        load_self,
        load_rec,
        load_exc,
    ) = loads

    pl.semaphore_wait(barrier, len(greeted))

    for device in row_peers:
        pl.semaphore_signal(row_sem, inc=1, device_id=device, device_id_type=MESH)
    load_newest.wait()
    load_cyc.wait()
    start_slot = newest_ref[0]
    newest_value = cyc[start_slot]
    load_all_rad.wait()
    partial_slab = lax.dot_general(rad[...], newest_value, dims, preferred_element_type=F32)
    for k in range(m):
        top, middle = k * rays, k * rays + rays // 2
        rs_send[k] = jnp.concatenate(
            [partial_slab[top:middle], partial_slab[middle : top + rays]], axis=1
        ).astype(BF16)
    slab_copies = ray_copies(lambda d: rs_send.at[other_ray(d)], rs_recv.at[r], 0)
    for copy in slab_copies:
        copy.start()
    rs_recv[r] = rs_send[r]
    cycle_copies = near_copies(cyc_hbm, nearby, 0)
    for copy in cycle_copies:
        copy.start()
    near_all = list(cycle_copies)

    load_list.wait()
    load_count.wait()
    near_shift = []
    near_valid = []
    for b in range(entries):
        shift = list_ref[0, b]
        source = g + shift - REACH
        near_shift.append(shift)
        near_valid.append((b < count_ref[0]) & (source >= 0) & (source < n))
    load_tr.wait()
    every = lax.broadcasted_iota(jnp.int32, (n, rays), 0)
    weights = tr[...]
    for b in range(entries):
        hit = near_valid[b] & (every == g + near_shift[b] - REACH)
        weights = jnp.where(hit, 0.0, weights)
    turned = weights.T
    w_rows = jnp.concatenate([turned[: rays // 2], turned[rays // 2 :]], axis=1)
    w_send[...] = w_rows.reshape(w_send.shape)

    pl.semaphore_wait(row_sem, len(row_peers))

    def send_weights(k):
        remote(
            w_send.at[k], w_recv.at[chunk], w_sems.at[0], w_sems.at[1], first_target + k, r
        ).start()

    each_target(send_weights, False)
    w_recv[chunk] = w_send[chunk]
    rad_copies = ray_copies(
        lambda d: rad_hbm.at[pl.ds(pl.multiple_of(other_ray(d) * rays, rays), rays), :],
        rad_full.at[:, mine],
        1,
    )
    inv_copies = ray_copies(lambda d: inv_hbm, inv_full.at[:, mine], 2)
    for copy in rad_copies + inv_copies:
        copy.start()
    rec_copies = ray_copies(lambda d: rec_hbm, rec_full.at[rows_here, :], 3)
    p_copies = []

    def send_slab(step, wide):
        for k in range(chunks):
            s_send[step, k] = wide[k * rows : (k + 1) * rows].astype(BF16)

        def send(group, k):
            remote(
                s_send.at[step, k],
                s_recv.at[step, g],
                s_sems.at[step, 0],
                s_sems.at[step, 1],
                group,
                r,
            ).start()

        each_peer(send)
        s_recv[step, g] = s_send[step, chunk]

    def fold(step):
        wait_blocks(s_recv.at[step], s_sems.at[step, 1])
        for h in range(n):
            turn_s[h * rows : (h + 1) * rows] = s_recv[step, h].astype(F32)
        lane = lax.broadcasted_iota(jnp.int32, (n, 2 * waves), 1)
        for i in range(rows):
            slab = turn_s[pl.ds(i, n, stride=rows), :]
            wide = jnp.concatenate(
                [jnp.where(lane < waves, slab, 0.0), jnp.where(lane < waves, 0.0, slab)], axis=0
            ).astype(BF16)
            both = jnp.dot(w_both[i], wide, preferred_element_type=F32)
            turn_f[i * chunks : (i + 1) * chunks] = both[:chunks] + both[chunks:]
        for k in range(chunks):
            f_send[step, k] = turn_f[pl.ds(k, rows, stride=chunks), :].astype(BF16)
        place = r * chunks + chunk

        def send(k, ray):
            remote(
                f_send.at[step, k],
                f_recv.at[step, place],
                f_sems.at[step, 0],
                f_sems.at[step, 1],
                first_target + k,
                ray,
            ).start()

        if step:
            for d in ray_order:
                each_target(lambda k, ray=other_ray(d): send(k, ray), True)
        each_target(lambda k: send(k, r), False)
        f_recv[step, place] = f_send[step, chunk]

    def send_partial(step, part):
        p_send[step] = part
        copies = [
            remote(
                p_send.at[step],
                p_recv.at[step, r],
                p_sems.at[step, 0, d - 1],
                p_sems.at[step, 1, d - 1],
                g,
                other_ray(d),
            )
            for d in ray_order
        ]
        for copy in copies:
            copy.start()
        p_copies.append(copies)
        p_recv[step, r] = part

    for copy in slab_copies:
        copy.wait_recv()
    first_slab = rs_recv[0].astype(F32)
    for k in range(1, m):
        first_slab = first_slab + rs_recv[k].astype(F32)
    send_slab(0, first_slab)

    load_self.wait()
    load_blocks.wait()
    load_exc.wait()
    for copy in cycle_copies:
        copy.wait_recv()
    base[...] = jnp.zeros_like(base)
    for step in range(steps):
        base[step, :, mine] = exc[step].astype(F32)

    def add_cycle(b, carry):
        shift = list_ref[0, b]
        source = g + shift - REACH
        valid = (b < count_ref[0]) & (source >= 0) & (source < n)
        past = [nearby[shift, lax.rem(start_slot - i + slots, slots)] for i in range(slots)]
        past = [jnp.where(valid, x, jnp.zeros_like(x)) for x in past]
        blank = jnp.zeros_like(past[0])
        lagged = jnp.concatenate(
            [
                jnp.concatenate([blank] * step + past[: slots - step], axis=1)
                for step in range(steps)
            ],
            axis=0,
        )
        near = jnp.dot(
            lagged, blocks[b].reshape(slots * width, size), preferred_element_type=F32
        )
        for step in range(steps):
            base[step] = base[step] - near[step * waves : (step + 1) * waves]
        return carry

    lax.fori_loop(0, entries, add_cycle, 0)

    wait_blocks(w_recv, w_sems.at[1])
    for i in range(rows):
        w_all = w_recv[:, i, :]
        w_high = w_all.astype(BF16)
        w_both[i, :chunks] = w_high
        w_both[i, chunks:] = (w_all - w_high.astype(F32)).astype(BF16)
    fold(0)

    load_rad.wait()
    load_inv.wait()
    load_own_inv.wait()
    for copy in rad_copies + inv_copies:
        copy.wait_recv()
    slab_of_drive[...] = lax.dot_general(
        rad_full[...], inv_full[...], dims, preferred_element_type=F32
    ).astype(BF16)

    def gathered_sum(step):
        for copy in p_copies[step]:
            copy.wait_recv()
        total = p_recv[step, 0].astype(F32)
        for d in range(1, m):
            total = total + p_recv[step, d].astype(F32)
        return total

    def turn_field(pieces):
        turned = jnp.concatenate([x.astype(F32) for x in pieces], axis=0).T.astype(BF16)
        span = rays // 2
        return jnp.concatenate(
            [
                turned[p * waves : (p + 1) * waves, k * span : (k + 1) * span]
                for k in range(len(pieces) // chunks)
                for p in range(2)
            ],
            axis=1,
        )

    for step in range(steps):
        if step == 0:
            load_rec.wait()
            wait_blocks(f_recv.at[0], f_sems.at[0, 1], chunks - 1)
            field = turn_field([f_recv[0, r * chunks + k] for k in range(chunks)])
            far = jnp.dot(field, rec_full[rows_here, :], preferred_element_type=F32)
            send_partial(0, (base[0] - far).astype(BF16))
            for copy in rec_copies:
                copy.start()
            drive = gathered_sum(0).astype(BF16)
        else:
            total = gathered_sum(step)
            if step == 1:
                for copy in rec_copies:
                    copy.wait_recv()
            wait_blocks(f_recv.at[step], f_sems.at[step, 1])
            field = turn_field([f_recv[step, k] for k in range(m * chunks)])
            far = jnp.dot(field, rec_full[...], preferred_element_type=F32)
            drive = (total - far).astype(BF16)
        if step + 1 < steps:
            slab = lax.dot_general(slab_of_drive[...], drive, dims, preferred_element_type=F32)
            send_slab(
                step + 1, jnp.concatenate([slab[: rays // 2], slab[rays // 2 :]], axis=1)
            )
        own[step] = jnp.dot(drive, inv[...], preferred_element_type=F32).astype(BF16)
        out_ref[step] = own[step]
        if step + 1 < steps:
            fresh = fresh_of[step]
            copies = near_copies(own.at[step], fresh, step + 1)
            for copy in copies:
                copy.start()
            near_all.extend(copies)
            fresh[REACH] = own[step]
            for copy in copies:
                copy.wait_recv()

            def add_near(later):
                latest = [fresh[near_shift[b]] for b in range(entries)]
                latest = [
                    jnp.where(near_valid[b], x, jnp.zeros_like(x)) for b, x in enumerate(latest)
                ]
                base[later] = base[later] - jnp.dot(
                    jnp.concatenate(latest, axis=1),
                    blocks[:, later - step - 1].reshape(entries * width, size),
                    preferred_element_type=F32,
                )

            add_near(step + 1)
            send_partial(step + 1, base[step + 1].astype(BF16))
            fold(step + 1)
            for later in range(step + 2, steps):
                add_near(later)

    for copy in slab_copies + rad_copies + inv_copies + rec_copies + near_all + sum(p_copies, []):
        copy.wait_send()
    wait_blocks(w_send, w_sems.at[0])
    for step in range(steps):
        wait_blocks(s_recv.at[step], s_sems.at[step, 0])
        wait_blocks(f_recv.at[step], f_sems.at[step, 0], None if step else chunks - 1)


def layout_of(n):
    inner = 1
    while inner * inner < n:
        inner *= 2
    return inner, max(n // (2 * inner), 1)


def solution(mesh):
    n = mesh.shape["groups"]
    m = mesh.shape["rays"]
    inner, copies_of_fold = layout_of(n)
    chunks = n // copies_of_fold

    def local(
        excitation,
        cycle,
        near_blocks,
        near_list,
        near_count,
        newest,
        inverse,
        radiate,
        translate,
        receive,
    ):
        steps, waves, width = excitation.shape
        slots = cycle.shape[0]
        entries = near_list.shape[1]
        size = m * width
        rays = receive.shape[0]
        rows = rays // (2 * chunks)
        spread = 2 * REACH + 1
        anywhere = pl.BlockSpec(memory_space=pl.ANY)
        dma = pltpu.SemaphoreType.DMA
        vmem = pltpu.VMEM
        smem = pltpu.SMEM
        return pl.pallas_call(
            functools.partial(kernel, n, inner, copies_of_fold, m),
            out_shape=jax.ShapeDtypeStruct(excitation.shape, BF16),
            in_specs=[anywhere] * 10,
            out_specs=pl.BlockSpec(memory_space=vmem),
            scratch_shapes=[
                smem(near_list.shape, jnp.int32),
                smem(near_count.shape, jnp.int32),
                smem(newest.shape, jnp.int32),
                vmem(excitation.shape, BF16),
                vmem(cycle.shape, BF16),
                vmem((entries, slots, width, size), BF16),
                vmem((n, rays), F32),
                vmem(radiate.shape, BF16),
                vmem(inverse.shape, BF16),
                vmem((m, rays // 2, 2 * waves), BF16),
                vmem((m, rays // 2, 2 * waves), BF16),
                vmem((rays, size), BF16),
                vmem((size, size), BF16),
                vmem((rays, size), BF16),
                vmem((m * rays, size), BF16),
                vmem((spread, slots, waves, width), BF16),
                vmem((spread, waves, width), BF16),
                vmem((spread, waves, width), BF16),
                vmem((chunks, rows, 2 * n), F32),
                vmem((chunks, rows, 2 * n), F32),
                vmem((rows, 2 * chunks, 2 * n), BF16),
                vmem((n * rows, 2 * waves), F32),
                vmem((chunks * rows, 2 * waves), F32),
                vmem((steps, chunks, rows, 2 * waves), BF16),
                vmem((steps, n, rows, 2 * waves), BF16),
                vmem((steps, chunks, rows, 2 * waves), BF16),
                vmem((steps, m * chunks, rows, 2 * waves), BF16),
                vmem((steps, waves, size), F32),
                vmem((steps, waves, size), BF16),
                vmem((steps, m, waves, size), BF16),
                vmem((steps, waves, width), BF16),
                pltpu.SemaphoreType.REGULAR,
                dma((13,)),
                dma((4, m - 1)),
                dma((4, m - 1)),
                dma((2,)),
                dma((steps, 2)),
                dma((steps, 2)),
                dma((steps, 4)),
                dma((steps, 4)),
                dma((steps, 2, m - 1)),
            ],
            compiler_params=pltpu.CompilerParams(
                collective_id=0, has_side_effects=True, vmem_limit_bytes=56 * 1024 * 1024
            ),
        )(
            excitation,
            cycle,
            near_blocks,
            near_list,
            near_count,
            newest,
            inverse,
            radiate,
            translate,
            receive,
        )

    placed = (
        P(None, None, ("groups", "rays")),
        P(None, None, ("groups", "rays")),
        P("groups", None, None, "rays", None),
        P("groups", None),
        P("groups"),
        P(),
        P(None, ("groups", "rays")),
        P(None, ("groups", "rays")),
        P("groups", None, "rays"),
        P("rays", "groups"),
    )
    return jax.shard_map(
        local,
        mesh=mesh,
        in_specs=placed,
        out_specs=P(None, None, ("groups", "rays")),
        check_vma=False,
    )
```

time: 387 us -> 67.6 us (0.17)
  waiting for transfers between devices: 238 us -> 0 us
  Pallas kernels: 0 us -> 65.4 us
  blocking collectives: 43.7 us -> 0 us
  starting transfers between devices: 37.9 us -> 0 us
  other arithmetic: 19.3 us -> 0 us
  between operations: 18.2 us -> 0.66 us
  matrix products: 16.6 us -> 0 us
  local copies, waits for them, and re-layouts: 10.6 us -> 1.42 us
    all_gather x3 -> x0, waiting for transfers between devices: 167 us -> none  [far_only(): return fold_far(lax.all_gather(slab[None], 'groups', axis=0, tiled=True))]
    reduce_scatter x3 -> x0, waiting for transfers between devices: 65.7 us -> none  [the longest x2 40.9 us: local(): lax.psum_scatter(aggregate_partial_value, 'rays', scatter_dimension=1, ti...]
    pallas_call x0 -> x1, Pallas kernels: none -> 65.4 us  [local(): pl.pallas_call(functools.partial(kernel, n, inner, copies_of_fold, m), ou...]
    psum x3 -> x0, blocking collectives: 43.7 us -> none  [local(): drive = lax.psum(term, 'rays').astype(jnp.bfloat16)]
    ppermute x12 -> x0, starting transfers between devices: 37.7 us -> none  [shifted(): return lax.ppermute(block, axis, route)]
    dot_general x15 -> x0, matrix products: 16.6 us -> none  [the longest x3 10.6 us: local(): near = jnp.dot(near_rows, blocks, preferred_element_type=jnp.float32)]
    unnamed x4 -> x0, other arithmetic: 7.73 us -> none
    ppermute x12 -> x0, waiting for transfers between devices: 5.68 us -> none  [shifted(): return lax.ppermute(block, axis, route)]
  transfers between devices with their start and end apart: 18 -> 0, of which waited for: 10 -> 0; matrix products, arithmetic and copies ran while one was open for 8% -> 0% of each run, Pallas kernels for 0% -> 0%
where the time goes in v1:
time: 67.6 us; the launch traced here: 67.5 us
  Pallas kernels  65.4 us (97%)
  local copies, waits for them, and re-layouts  1.42 us (2%)
    pallas_call x1, Pallas kernels, local(): pl.pallas_call(functools.partial(kernel, n, inner, copies_of_fold, m), ou...  65.4 us
    unnamed x1, local copies, waits for them, and re-layouts  1.42 us

profile of v1, /device:TPU:1, one launch (start us, length us, event | category | flops | bytes accessed | tf_op | source)
XLA Modules:
  0.0 67.5 jit_solution(2499903711551722760)
XLA Ops:
  0.7 65.4 %shard_map.100 = bf16[3,64,128]{2,1,0:T(8,128)(2,1)} custom-call(bf16[3,64,128]{2,1,0:T(8,128)(2,1)} %exc_hbm.1, bf16[8,64,128]{2,1,0:T(8,128)(2,1)} %cyc_hbm.1, bf16[1,5,8,128,512]{4,3,2,1,0:T(8,128)(2,1)} %blocks_hbm.1, s32[1,5]{1,0:T(1,128)} %list_hbm.1, s32[1]{0:T(128)S(6)} %copy.12.count_hbm, s32[8]{0:T(128)} %newest_hbm.1, bf16[512,128]{1,0:T(8,128)(2,1)} %inv_hbm.1, ...), custom_call_target="tpu_custom_call" | custom-call | tf_op jit(solution)/shard_map/pallas_call | solution.py:515
  66.1 1.4 %copy.13 = bf16[3,64,128]{2,1,0:T(8,128)(2,1)} copy(bf16[3,64,128]{2,1,0:T(8,128)(2,1)} %shard_map.100) | data formatting | bytes 98304

commit v2 on v1

--- a/solution.py
+++ b/solution.py
@@ -266,10 +266,47 @@
         rad_full.at[:, mine],
         1,
     )
-    inv_copies = ray_copies(lambda d: inv_hbm, inv_full.at[:, mine], 2)
-    for copy in rad_copies + inv_copies:
+    for copy in rad_copies:
         copy.start()
-    rec_copies = ray_copies(lambda d: rec_hbm, rec_full.at[rows_here, :], 3)
+
+    near_rays = sorted({1 % m, m - 1} - {0})
+
+    def columns_of(ray):
+        return pl.ds(pl.multiple_of(ray * width, width), width)
+
+    def rows_of(ray, half):
+        start = ray * rays + half * (rays // 2)
+        return pl.ds(pl.multiple_of(start, rays // 2), rays // 2)
+
+    def neighbour_copies(src, dst, index):
+        return [
+            remote(src, dst, x_send.at[index, d - 1], x_recv.at[index, d - 1], g, other_ray(d))
+            for d in near_rays
+        ]
+
+    def pass_copies(part_of, index):
+        if m != 4:
+            return []
+        return [
+            remote(
+                part_of(other_ray(m - d), k),
+                part_of(other_ray(m - d), k),
+                x_send.at[index, d - 1],
+                x_recv.at[index, d - 1],
+                g,
+                other_ray(d),
+            )
+            for k, d in enumerate(near_rays)
+        ]
+
+    inv_copies = neighbour_copies(inv_hbm, inv_full.at[:, mine], 2)
+    rec_copies = neighbour_copies(rec_hbm, rec_full.at[rows_here, :], 3)
+    inv_passed = pass_copies(
+        lambda ray, k: inv_full.at[pl.ds(k * (size // 2), size // 2), columns_of(ray)], 4
+    )
+    rec_passed = pass_copies(lambda ray, k: rec_full.at[rows_of(ray, k), :], 5)
+    for copy in inv_copies:
+        copy.start()
     p_copies = []
 
     def send_slab(step, wide):
@@ -377,6 +414,12 @@
         return carry
 
     lax.fori_loop(0, entries, add_cycle, 0)
+    for copy in rec_copies:
+        copy.start()
+    for copy in inv_copies:
+        copy.wait_recv()
+    for copy in inv_passed:
+        copy.start()
 
     wait_blocks(w_recv, w_sems.at[1])
     for i in range(rows):
@@ -389,7 +432,7 @@
     load_rad.wait()
     load_inv.wait()
     load_own_inv.wait()
-    for copy in rad_copies + inv_copies:
+    for copy in rad_copies + inv_passed:
         copy.wait_recv()
     slab_of_drive[...] = lax.dot_general(
         rad_full[...], inv_full[...], dims, preferred_element_type=F32
@@ -423,12 +466,14 @@
             far = jnp.dot(field, rec_full[rows_here, :], preferred_element_type=F32)
             send_partial(0, (base[0] - far).astype(BF16))
             for copy in rec_copies:
+                copy.wait_recv()
+            for copy in rec_passed:
                 copy.start()
             drive = gathered_sum(0).astype(BF16)
         else:
             total = gathered_sum(step)
             if step == 1:
-                for copy in rec_copies:
+                for copy in rec_passed:
                     copy.wait_recv()
             wait_blocks(f_recv.at[step], f_sems.at[step, 1])
             field = turn_field([f_recv[step, k] for k in range(m * chunks)])
@@ -468,7 +513,8 @@
             for later in range(step + 2, steps):
                 add_near(later)
 
-    for copy in slab_copies + rad_copies + inv_copies + rec_copies + near_all + sum(p_copies, []):
+    gathers = inv_copies + rec_copies + inv_passed + rec_passed
+    for copy in slab_copies + rad_copies + gathers + near_all + sum(p_copies, []):
         copy.wait_send()
     wait_blocks(w_send, w_sems.at[0])
     for step in range(steps):
@@ -551,8 +597,8 @@
                 vmem((steps, waves, width), BF16),
                 pltpu.SemaphoreType.REGULAR,
                 dma((13,)),
-                dma((4, m - 1)),
-                dma((4, m - 1)),
+                dma((6, m - 1)),
+                dma((6, m - 1)),
                 dma((2,)),
                 dma((steps, 2)),
                 dma((steps, 2)),

time: 67.6 us -> 69.1 us (1.022)
  Pallas kernels: 65.4 us -> 66.9 us
    pallas_call x1, Pallas kernels: 65.4 us -> 66.9 us  [local(): pl.pallas_call(functools.partial(kernel, n, inner, copies_of_fold, m), ou...]
where the time goes in v2:
time: 69.1 us; the launch traced here: 69 us
  Pallas kernels  66.9 us (97%)
  local copies, waits for them, and re-layouts  1.42 us (2%)
    pallas_call x1, Pallas kernels, local(): pl.pallas_call(functools.partial(kernel, n, inner, copies_of_fold, m), ou...  66.9 us
    unnamed x1, local copies, waits for them, and re-layouts  1.42 us

profile of v2, /device:TPU:1, one launch (start us, length us, event | category | flops | bytes accessed | tf_op | source)
XLA Modules:
  0.0 69.0 jit_solution(14730587740692097321)
XLA Ops:
  0.7 66.9 %shard_map.100 = bf16[3,64,128]{2,1,0:T(8,128)(2,1)} custom-call(bf16[3,64,128]{2,1,0:T(8,128)(2,1)} %exc_hbm.1, bf16[8,64,128]{2,1,0:T(8,128)(2,1)} %cyc_hbm.1, bf16[1,5,8,128,512]{4,3,2,1,0:T(8,128)(2,1)} %blocks_hbm.1, s32[1,5]{1,0:T(1,128)} %list_hbm.1, s32[1]{0:T(128)S(6)} %copy.12.count_hbm, s32[8]{0:T(128)} %newest_hbm.1, bf16[512,128]{1,0:T(8,128)(2,1)} %inv_hbm.1, ...), custom_call_target="tpu_custom_call" | custom-call | tf_op jit(solution)/shard_map/pallas_call | solution.py:561
  67.6 1.4 %copy.13 = bf16[3,64,128]{2,1,0:T(8,128)(2,1)} copy(bf16[3,64,128]{2,1,0:T(8,128)(2,1)} %shard_map.100) | data formatting | bytes 98304

commit v3 on v1

--- a/solution.py
+++ b/solution.py
@@ -163,15 +163,6 @@
             for d in ray_order
         ]
 
-    barrier = pltpu.get_barrier_semaphore()
-    greeted = [(g, other_ray(d)) for d in ray_order]
-    greeted += [(go * inner + inner_place[d], r) for d in inner_order if d]
-    row_peers = [(wrap(go + d, outer) * inner + gi, r) for d in range(1, outer)]
-    greeted += row_peers
-    greeted += [(near_group(d), r) for d in NEAR_SHIFTS]
-    for device in greeted:
-        pl.semaphore_signal(barrier, inc=1, device_id=device, device_id_type=MESH)
-
     rows_here = pl.ds(pl.multiple_of(r * rays, rays), rays)
     pairs = (
         (newest_hbm, newest_ref),
@@ -191,7 +182,19 @@
     loads = [
         pltpu.make_async_copy(src, dst, load_sems.at[i]) for i, (src, dst) in enumerate(pairs)
     ]
-    for load in loads:
+    for load in loads[:3]:
+        load.start()
+
+    barrier = pltpu.get_barrier_semaphore()
+    greeted = [(g, other_ray(d)) for d in ray_order]
+    greeted += [(go * inner + inner_place[d], r) for d in inner_order if d]
+    row_peers = [(wrap(go + d, outer) * inner + gi, r) for d in range(1, outer)]
+    greeted += row_peers
+    greeted += [(near_group(d), r) for d in NEAR_SHIFTS]
+    for device in greeted:
+        pl.semaphore_signal(barrier, inc=1, device_id=device, device_id_type=MESH)
+
+    for load in loads[3:]:
         load.start()
     (
         load_newest,
@@ -376,7 +379,8 @@
             base[step] = base[step] - near[step * waves : (step + 1) * waves]
         return carry
 
-    lax.fori_loop(0, entries, add_cycle, 0)
+    early = (entries + 1) // 2
+    lax.fori_loop(0, early, add_cycle, 0)
 
     wait_blocks(w_recv, w_sems.at[1])
     for i in range(rows):
@@ -386,14 +390,7 @@
         w_both[i, chunks:] = (w_all - w_high.astype(F32)).astype(BF16)
     fold(0)
 
-    load_rad.wait()
-    load_inv.wait()
-    load_own_inv.wait()
-    for copy in rad_copies + inv_copies:
-        copy.wait_recv()
-    slab_of_drive[...] = lax.dot_general(
-        rad_full[...], inv_full[...], dims, preferred_element_type=F32
-    ).astype(BF16)
+    lax.fori_loop(early, entries, add_cycle, 0)
 
     def gathered_sum(step):
         for copy in p_copies[step]:
@@ -424,6 +421,14 @@
             send_partial(0, (base[0] - far).astype(BF16))
             for copy in rec_copies:
                 copy.start()
+            load_rad.wait()
+            load_inv.wait()
+            load_own_inv.wait()
+            for copy in rad_copies + inv_copies:
+                copy.wait_recv()
+            slab_of_drive[...] = lax.dot_general(
+                rad_full[...], inv_full[...], dims, preferred_element_type=F32
+            ).astype(BF16)
             drive = gathered_sum(0).astype(BF16)
         else:
             total = gathered_sum(step)
@@ -434,20 +439,21 @@
             field = turn_field([f_recv[step, k] for k in range(m * chunks)])
             far = jnp.dot(field, rec_full[...], preferred_element_type=F32)
             drive = (total - far).astype(BF16)
+        current = jnp.dot(drive, inv[...], preferred_element_type=F32).astype(BF16)
         if step + 1 < steps:
             slab = lax.dot_general(slab_of_drive[...], drive, dims, preferred_element_type=F32)
-            send_slab(
-                step + 1, jnp.concatenate([slab[: rays // 2], slab[rays // 2 :]], axis=1)
-            )
-        own[step] = jnp.dot(drive, inv[...], preferred_element_type=F32).astype(BF16)
-        out_ref[step] = own[step]
+            wide = jnp.concatenate([slab[: rays // 2], slab[rays // 2 :]], axis=1)
+        own[step] = current
         if step + 1 < steps:
             fresh = fresh_of[step]
             copies = near_copies(own.at[step], fresh, step + 1)
             for copy in copies:
                 copy.start()
             near_all.extend(copies)
-            fresh[REACH] = own[step]
+            send_slab(step + 1, wide)
+            fresh[REACH] = current
+        out_ref[step] = current
+        if step + 1 < steps:
             for copy in copies:
                 copy.wait_recv()
 
@@ -514,7 +520,7 @@
         smem = pltpu.SMEM
         return pl.pallas_call(
             functools.partial(kernel, n, inner, copies_of_fold, m),
-            out_shape=jax.ShapeDtypeStruct(excitation.shape, BF16),
+            out_shape=pltpu.VMEM(excitation.shape, BF16),
             in_specs=[anywhere] * 10,
             out_specs=pl.BlockSpec(memory_space=vmem),
             scratch_shapes=[

time: 67.6 us -> 65 us (0.962)
  Pallas kernels: 65.4 us -> 63.6 us
  local copies, waits for them, and re-layouts: 1.42 us -> 0.62 us
    pallas_call x1, Pallas kernels: 65.4 us -> 63.6 us  [local(): pl.pallas_call(functools.partial(kernel, n, inner, copies_of_fold, m), ou...]
    unnamed x1, local copies, waits for them, and re-layouts: 1.42 us -> 0.62 us
where the time goes in v3:
time: 65 us; the launch traced here: 64.9 us
  Pallas kernels  63.6 us (98%)
  between operations  0.66 us (1%)
    pallas_call x1, Pallas kernels, local(): pl.pallas_call(functools.partial(kernel, n, inner, copies_of_fold, m), ou...  63.6 us

profile of v3, /device:TPU:1, one launch (start us, length us, event | category | flops | bytes accessed | tf_op | source)
XLA Modules:
  0.0 64.9 jit_solution(320868384220813727)
XLA Ops:
  0.7 63.6 %shard_map.100 = bf16[3,64,128]{2,1,0:T(8,128)(2,1)S(1)} custom-call(bf16[3,64,128]{2,1,0:T(8,128)(2,1)} %exc_hbm.1, bf16[8,64,128]{2,1,0:T(8,128)(2,1)} %cyc_hbm.1, bf16[1,5,8,128,512]{4,3,2,1,0:T(8,128)(2,1)} %blocks_hbm.1, s32[1,5]{1,0:T(1,128)} %list_hbm.1, s32[1]{0:T(128)S(6)} %copy.13.count_hbm, s32[8]{0:T(128)} %newest_hbm.1, ...), custom_call_target="tpu_custom_call" | custom-call | tf_op jit(solution)/shard_map/pallas_call | solution.py:521
  64.3 0.6 copy.12

commit v4 on v3

--- a/solution.py
+++ b/solution.py
@@ -195,7 +195,7 @@
         pl.semaphore_signal(barrier, inc=1, device_id=device, device_id_type=MESH)
 
     for load in loads[3:]:
-        load.start()
+        load.start(priority=1)
     (
         load_newest,
         load_cyc,
@@ -232,8 +232,6 @@
         copy.start()
     rs_recv[r] = rs_send[r]
     cycle_copies = near_copies(cyc_hbm, nearby, 0)
-    for copy in cycle_copies:
-        copy.start()
     near_all = list(cycle_copies)
 
     load_list.wait()
@@ -270,9 +268,15 @@
         1,
     )
     inv_copies = ray_copies(lambda d: inv_hbm, inv_full.at[:, mine], 2)
-    for copy in rad_copies + inv_copies:
-        copy.start()
-    rec_copies = ray_copies(lambda d: rec_hbm, rec_full.at[rows_here, :], 3)
+    half = rays // 2
+    rec_copies = []
+    for k in range(2):
+        there = pl.ds(pl.multiple_of(r * rays + k * half, half), half)
+        rec_copies.append(
+            ray_copies(
+                lambda d, k=k: rec_hbm.at[pl.ds(k * half, half), :], rec_full.at[there, :], 3 + k
+            )
+        )
     p_copies = []
 
     def send_slab(step, wide):
@@ -348,6 +352,16 @@
     for k in range(1, m):
         first_slab = first_slab + rs_recv[k].astype(F32)
     send_slab(0, first_slab)
+    for copy in cycle_copies + rad_copies + inv_copies:
+        copy.start()
+
+    wait_blocks(w_recv, w_sems.at[1])
+    for i in range(rows):
+        w_all = w_recv[:, i, :]
+        w_high = w_all.astype(BF16)
+        w_both[i, :chunks] = w_high
+        w_both[i, chunks:] = (w_all - w_high.astype(F32)).astype(BF16)
+    fold(0)
 
     load_self.wait()
     load_blocks.wait()
@@ -379,18 +393,8 @@
             base[step] = base[step] - near[step * waves : (step + 1) * waves]
         return carry
 
-    early = (entries + 1) // 2
-    lax.fori_loop(0, early, add_cycle, 0)
-
-    wait_blocks(w_recv, w_sems.at[1])
-    for i in range(rows):
-        w_all = w_recv[:, i, :]
-        w_high = w_all.astype(BF16)
-        w_both[i, :chunks] = w_high
-        w_both[i, chunks:] = (w_all - w_high.astype(F32)).astype(BF16)
-    fold(0)
-
-    lax.fori_loop(early, entries, add_cycle, 0)
+
+    lax.fori_loop(0, entries, add_cycle, 0)
 
     def gathered_sum(step):
         for copy in p_copies[step]:
@@ -419,7 +423,7 @@
             field = turn_field([f_recv[0, r * chunks + k] for k in range(chunks)])
             far = jnp.dot(field, rec_full[rows_here, :], preferred_element_type=F32)
             send_partial(0, (base[0] - far).astype(BF16))
-            for copy in rec_copies:
+            for copy in rec_copies[0]:
                 copy.start()
             load_rad.wait()
             load_inv.wait()
@@ -433,7 +437,7 @@
         else:
             total = gathered_sum(step)
             if step == 1:
-                for copy in rec_copies:
+                for copy in rec_copies[0] + rec_copies[1]:
                     copy.wait_recv()
             wait_blocks(f_recv.at[step], f_sems.at[step, 1])
             field = turn_field([f_recv[step, k] for k in range(m * chunks)])
@@ -451,6 +455,9 @@
                 copy.start()
             near_all.extend(copies)
             send_slab(step + 1, wide)
+            if step == 0:
+                for copy in rec_copies[1]:
+                    copy.start()
             fresh[REACH] = current
         out_ref[step] = current
         if step + 1 < steps:
@@ -474,7 +481,7 @@
             for later in range(step + 2, steps):
                 add_near(later)
 
-    for copy in slab_copies + rad_copies + inv_copies + rec_copies + near_all + sum(p_copies, []):
+    for copy in slab_copies + rad_copies + inv_copies + sum(rec_copies, []) + near_all + sum(p_copies, []):
         copy.wait_send()
     wait_blocks(w_send, w_sems.at[0])
     for step in range(steps):
@@ -557,8 +564,8 @@
                 vmem((steps, waves, width), BF16),
                 pltpu.SemaphoreType.REGULAR,
                 dma((13,)),
-                dma((4, m - 1)),
-                dma((4, m - 1)),
+                dma((5, m - 1)),
+                dma((5, m - 1)),
                 dma((2,)),
                 dma((steps, 2)),
                 dma((steps, 2)),

time: 65 us -> 63.4 us (0.975)
  Pallas kernels: 63.6 us -> 62 us
    pallas_call x1, Pallas kernels: 63.6 us -> 62 us  [local(): pl.pallas_call(functools.partial(kernel, n, inner, copies_of_fold, m), ou...]
where the time goes in v4:
time: 63.4 us; the launch traced here: 63.3 us
  Pallas kernels  62 us (98%)
  between operations  0.66 us (1%)
    pallas_call x1, Pallas kernels, local(): pl.pallas_call(functools.partial(kernel, n, inner, copies_of_fold, m), ou...  62 us

profile of v4, /device:TPU:1, one launch (start us, length us, event | category | flops | bytes accessed | tf_op | source)
XLA Modules:
  0.0 63.3 jit_solution(4985430182396700217)
XLA Ops:
  0.7 62.0 %shard_map.100 = bf16[3,64,128]{2,1,0:T(8,128)(2,1)S(1)} custom-call(bf16[3,64,128]{2,1,0:T(8,128)(2,1)} %exc_hbm.1, bf16[8,64,128]{2,1,0:T(8,128)(2,1)} %cyc_hbm.1, bf16[1,5,8,128,512]{4,3,2,1,0:T(8,128)(2,1)} %blocks_hbm.1, s32[1,5]{1,0:T(1,128)} %list_hbm.1, s32[1]{0:T(128)S(6)} %copy.13.count_hbm, s32[8]{0:T(128)} %newest_hbm.1, ...), custom_call_target="tpu_custom_call" | custom-call | tf_op jit(solution)/shard_map/pallas_call | solution.py:528
  62.7 0.6 copy.12

commit v5 on v4

--- a/solution.py
+++ b/solution.py
@@ -267,16 +267,47 @@
         rad_full.at[:, mine],
         1,
     )
-    inv_copies = ray_copies(lambda d: inv_hbm, inv_full.at[:, mine], 2)
+    near_rays = sorted({1 % m, m - 1} - {0})
     half = rays // 2
-    rec_copies = []
-    for k in range(2):
-        there = pl.ds(pl.multiple_of(r * rays + k * half, half), half)
-        rec_copies.append(
-            ray_copies(
-                lambda d, k=k: rec_hbm.at[pl.ds(k * half, half), :], rec_full.at[there, :], 3 + k
+
+    def columns_of(ray):
+        return pl.ds(pl.multiple_of(ray * width, width), width)
+
+    def rows_of(ray, k):
+        return pl.ds(pl.multiple_of(ray * rays + k * half, half), half)
+
+    def ring_copies(part_of, index):
+        copies = []
+        for k, d in enumerate(near_rays):
+            src, dst = part_of(d, k)
+            copies.append(
+                remote(src, dst, x_send.at[index, d - 1], x_recv.at[index, d - 1], g, other_ray(d))
             )
-        )
+        return copies
+
+    def inv_part(d, k):
+        part = inv_full.at[pl.ds(k * (size // 2), size // 2), columns_of(other_ray(m - d))]
+        return part, part
+
+    def rec_part(d, k):
+        part = rec_full.at[rows_of(other_ray(m - d), k), :]
+        return part, part
+
+    inv_copies = ring_copies(lambda d, k: (inv_hbm, inv_full.at[:, mine]), 2)
+    inv_passed = ring_copies(inv_part, 3) if m == 4 else []
+    rec_copies = [
+        ring_copies(
+            lambda d, k: (rec_hbm.at[pl.ds(k * half, half), :], rec_full.at[rows_of(r, k), :]), 4
+        ),
+        ring_copies(
+            lambda d, k: (
+                rec_hbm.at[pl.ds((1 - k) * half, half), :],
+                rec_full.at[rows_of(r, 1 - k), :],
+            ),
+            5,
+        ),
+    ]
+    rec_passed = ring_copies(rec_part, 6) if m == 4 else []
     p_copies = []
 
     def send_slab(step, wide):
@@ -352,7 +383,7 @@
     for k in range(1, m):
         first_slab = first_slab + rs_recv[k].astype(F32)
     send_slab(0, first_slab)
-    for copy in cycle_copies + rad_copies + inv_copies:
+    for copy in cycle_copies + inv_copies + rad_copies:
         copy.start()
 
     wait_blocks(w_recv, w_sems.at[1])
@@ -362,6 +393,10 @@
         w_both[i, :chunks] = w_high
         w_both[i, chunks:] = (w_all - w_high.astype(F32)).astype(BF16)
     fold(0)
+    for copy in inv_copies:
+        copy.wait_recv()
+    for copy in inv_passed:
+        copy.start()
 
     load_self.wait()
     load_blocks.wait()
@@ -428,7 +463,7 @@
             load_rad.wait()
             load_inv.wait()
             load_own_inv.wait()
-            for copy in rad_copies + inv_copies:
+            for copy in rad_copies + inv_passed:
                 copy.wait_recv()
             slab_of_drive[...] = lax.dot_general(
                 rad_full[...], inv_full[...], dims, preferred_element_type=F32
@@ -437,7 +472,7 @@
         else:
             total = gathered_sum(step)
             if step == 1:
-                for copy in rec_copies[0] + rec_copies[1]:
+                for copy in rec_copies[1] + rec_passed:
                     copy.wait_recv()
             wait_blocks(f_recv.at[step], f_sems.at[step, 1])
             field = turn_field([f_recv[step, k] for k in range(m * chunks)])
@@ -456,7 +491,9 @@
             near_all.extend(copies)
             send_slab(step + 1, wide)
             if step == 0:
-                for copy in rec_copies[1]:
+                for copy in rec_copies[0]:
+                    copy.wait_recv()
+                for copy in rec_passed + rec_copies[1]:
                     copy.start()
             fresh[REACH] = current
         out_ref[step] = current
@@ -481,7 +518,8 @@
             for later in range(step + 2, steps):
                 add_near(later)
 
-    for copy in slab_copies + rad_copies + inv_copies + sum(rec_copies, []) + near_all + sum(p_copies, []):
+    ringed = inv_copies + inv_passed + sum(rec_copies, rec_passed)
+    for copy in slab_copies + rad_copies + ringed + near_all + sum(p_copies, []):
         copy.wait_send()
     wait_blocks(w_send, w_sems.at[0])
     for step in range(steps):
@@ -564,8 +602,8 @@
                 vmem((steps, waves, width), BF16),
                 pltpu.SemaphoreType.REGULAR,
                 dma((13,)),
-                dma((5, m - 1)),
-                dma((5, m - 1)),
+                dma((7, m - 1)),
+                dma((7, m - 1)),
                 dma((2,)),
                 dma((steps, 2)),
                 dma((steps, 2)),

time: 63.4 us -> 62.9 us (level)
  no operation moved by 1% of the time
where the time goes in v5:
time: 62.9 us; the launch traced here: 62.8 us
  Pallas kernels  61.5 us (98%)
  between operations  0.66 us (1%)
    pallas_call x1, Pallas kernels, local(): pl.pallas_call(functools.partial(kernel, n, inner, copies_of_fold, m), ou...  61.5 us

profile of v5, /device:TPU:1, one launch (start us, length us, event | category | flops | bytes accessed | tf_op | source)
XLA Modules:
  0.0 62.8 jit_solution(15978082559775545083)
XLA Ops:
  0.7 61.5 %shard_map.100 = bf16[3,64,128]{2,1,0:T(8,128)(2,1)S(1)} custom-call(bf16[3,64,128]{2,1,0:T(8,128)(2,1)} %exc_hbm.1, bf16[8,64,128]{2,1,0:T(8,128)(2,1)} %cyc_hbm.1, bf16[1,5,8,128,512]{4,3,2,1,0:T(8,128)(2,1)} %blocks_hbm.1, s32[1,5]{1,0:T(1,128)} %list_hbm.1, s32[1]{0:T(128)S(6)} %copy.13.count_hbm, s32[8]{0:T(128)} %newest_hbm.1, ...), custom_call_target="tpu_custom_call" | custom-call | tf_op jit(solution)/shard_map/pallas_call | solution.py:566
  62.2 0.6 copy.12

commit v6 on v5

--- a/solution.py
+++ b/solution.py
@@ -348,7 +348,7 @@
                 f_send.at[step, k],
                 f_recv.at[step, place],
                 f_sems.at[step, 0],
-                f_sems.at[step, 1],
+                f_sems.at[step, 1 + r],
                 first_target + k,
                 ray,
             ).start()
@@ -407,29 +407,39 @@
     for step in range(steps):
         base[step, :, mine] = exc[step].astype(F32)
 
-    def add_cycle(b, carry):
+    def add_cycle(b, first, last):
         shift = list_ref[0, b]
         source = g + shift - REACH
         valid = (b < count_ref[0]) & (source >= 0) & (source < n)
-        past = [nearby[shift, lax.rem(start_slot - i + slots, slots)] for i in range(slots)]
+        past = [
+            nearby[shift, lax.rem(start_slot - i + slots, slots)] for i in range(slots - first)
+        ]
         past = [jnp.where(valid, x, jnp.zeros_like(x)) for x in past]
         blank = jnp.zeros_like(past[0])
         lagged = jnp.concatenate(
             [
-                jnp.concatenate([blank] * step + past[: slots - step], axis=1)
-                for step in range(steps)
+                jnp.concatenate([blank] * k + past[: len(past) - k], axis=1)
+                for k in range(last - first)
             ],
             axis=0,
         )
         near = jnp.dot(
-            lagged, blocks[b].reshape(slots * width, size), preferred_element_type=F32
+            lagged,
+            blocks[b, first:].reshape((slots - first) * width, size),
+            preferred_element_type=F32,
         )
-        for step in range(steps):
-            base[step] = base[step] - near[step * waves : (step + 1) * waves]
+        for k in range(last - first):
+            base[first + k] = base[first + k] - near[k * waves : (k + 1) * waves]
+
+    def add_first(b, carry):
+        add_cycle(b, 0, 1)
         return carry
 
-
-    lax.fori_loop(0, entries, add_cycle, 0)
+    def add_later(b, carry):
+        add_cycle(b, 1, steps)
+        return carry
+
+    lax.fori_loop(0, entries, add_first, 0)
 
     def gathered_sum(step):
         for copy in p_copies[step]:
@@ -454,7 +464,7 @@
     for step in range(steps):
         if step == 0:
             load_rec.wait()
-            wait_blocks(f_recv.at[0], f_sems.at[0, 1], chunks - 1)
+            wait_blocks(f_recv.at[0], f_sems.at[0, 1 + r], chunks - 1)
             field = turn_field([f_recv[0, r * chunks + k] for k in range(chunks)])
             far = jnp.dot(field, rec_full[rows_here, :], preferred_element_type=F32)
             send_partial(0, (base[0] - far).astype(BF16))
@@ -468,16 +478,24 @@
             slab_of_drive[...] = lax.dot_general(
                 rad_full[...], inv_full[...], dims, preferred_element_type=F32
             ).astype(BF16)
+            lax.fori_loop(0, entries, add_later, 0)
             drive = gathered_sum(0).astype(BF16)
         else:
             total = gathered_sum(step)
             if step == 1:
                 for copy in rec_copies[1] + rec_passed:
                     copy.wait_recv()
-            wait_blocks(f_recv.at[step], f_sems.at[step, 1])
-            field = turn_field([f_recv[step, k] for k in range(m * chunks)])
-            far = jnp.dot(field, rec_full[...], preferred_element_type=F32)
-            drive = (total - far).astype(BF16)
+            for d in ray_order + [0]:
+                plane_ray = other_ray(d)
+                wait_blocks(
+                    f_recv.at[step], f_sems.at[step, 1 + plane_ray], chunks if d else chunks - 1
+                )
+                field = turn_field([f_recv[step, plane_ray * chunks + k] for k in range(chunks)])
+                start = pl.multiple_of(plane_ray * rays, rays)
+                total = total - jnp.dot(
+                    field, rec_full[pl.ds(start, rays), :], preferred_element_type=F32
+                )
+            drive = total.astype(BF16)
         current = jnp.dot(drive, inv[...], preferred_element_type=F32).astype(BF16)
         if step + 1 < steps:
             slab = lax.dot_general(slab_of_drive[...], drive, dims, preferred_element_type=F32)
@@ -606,7 +624,7 @@
                 dma((7, m - 1)),
                 dma((2,)),
                 dma((steps, 2)),
-                dma((steps, 2)),
+                dma((steps, 1 + m)),
                 dma((steps, 4)),
                 dma((steps, 4)),
                 dma((steps, 2, m - 1)),

time: 62.9 us -> 64.1 us (1.019)
  Pallas kernels: 61.5 us -> 62.8 us
    pallas_call x1, Pallas kernels: 61.5 us -> 62.8 us  [local(): pl.pallas_call(functools.partial(kernel, n, inner, copies_of_fold, m), ou...]
where the time goes in v6:
time: 64.1 us
  Pallas kernels  62.8 us (98%)
  between operations  0.66 us (1%)
    pallas_call x1, Pallas kernels, local(): pl.pallas_call(functools.partial(kernel, n, inner, copies_of_fold, m), ou...  62.8 us

profile of v6, /device:TPU:1, one launch (start us, length us, event | category | flops | bytes accessed | tf_op | source)
XLA Modules:
  0.0 64.1 jit_solution(10433567223863458441)
XLA Ops:
  0.7 62.8 %shard_map.100 = bf16[3,64,128]{2,1,0:T(8,128)(2,1)S(1)} custom-call(bf16[3,64,128]{2,1,0:T(8,128)(2,1)} %exc_hbm.1, bf16[8,64,128]{2,1,0:T(8,128)(2,1)} %cyc_hbm.1, bf16[1,5,8,128,512]{4,3,2,1,0:T(8,128)(2,1)} %blocks_hbm.1, s32[1,5]{1,0:T(1,128)} %list_hbm.1, s32[1]{0:T(128)S(6)} %copy.13.count_hbm, s32[8]{0:T(128)} %newest_hbm.1, ...), custom_call_target="tpu_custom_call" | custom-call | tf_op jit(solution)/shard_map/pallas_call | solution.py:584
  63.4 0.6 copy.12

commit v7 on v5

--- a/solution.py
+++ b/solution.py
@@ -45,6 +45,8 @@
     inv_full,
     slab_of_drive,
     rec_full,
+    slab_of_field,
+    current_of_field,
     nearby,
     fresh_first,
     fresh_second,
@@ -221,16 +223,17 @@
     start_slot = newest_ref[0]
     newest_value = cyc[start_slot]
     load_all_rad.wait()
-    partial_slab = lax.dot_general(rad[...], newest_value, dims, preferred_element_type=F32)
-    for k in range(m):
-        top, middle = k * rays, k * rays + rays // 2
-        rs_send[k] = jnp.concatenate(
-            [partial_slab[top:middle], partial_slab[middle : top + rays]], axis=1
-        ).astype(BF16)
     slab_copies = ray_copies(lambda d: rs_send.at[other_ray(d)], rs_recv.at[r], 0)
-    for copy in slab_copies:
-        copy.start()
-    rs_recv[r] = rs_send[r]
+    for d, copy in zip(ray_order + [0], slab_copies + [None]):
+        ray = other_ray(d)
+        block = rad[pl.ds(pl.multiple_of(ray * rays, rays), rays), :]
+        block = lax.dot_general(block, newest_value, dims, preferred_element_type=F32)
+        block = jnp.concatenate([block[: rays // 2], block[rays // 2 :]], axis=1).astype(BF16)
+        if copy is None:
+            rs_recv[r] = block
+        else:
+            rs_send[ray] = block
+            copy.start()
     cycle_copies = near_copies(cyc_hbm, nearby, 0)
     near_all = list(cycle_copies)
 
@@ -353,9 +356,15 @@
                 ray,
             ).start()
 
-        if step:
-            for d in ray_order:
-                each_target(lambda k, ray=other_ray(d): send(k, ray), True)
+        if step and m > 1:
+
+            def body(k, carry):
+                d = jnp.where(k == 0, m // 2, jnp.where(k == 1, 1, m - 1))
+                ray = wrap(r + d, m)
+                each_target(lambda k: send(k, ray), True)
+                return carry
+
+            lax.fori_loop(0, m - 1, body, 0)
         each_target(lambda k: send(k, r), False)
         f_recv[step, place] = f_send[step, chunk]
 
@@ -452,6 +461,7 @@
         )
 
     for step in range(steps):
+        more = step + 1 < steps
         if step == 0:
             load_rec.wait()
             wait_blocks(f_recv.at[0], f_sems.at[0, 1], chunks - 1)
@@ -469,18 +479,32 @@
                 rad_full[...], inv_full[...], dims, preferred_element_type=F32
             ).astype(BF16)
             drive = gathered_sum(0).astype(BF16)
+            current = jnp.dot(drive, inv[...], preferred_element_type=F32).astype(BF16)
+            slab = lax.dot_general(slab_of_drive[...], drive, dims, preferred_element_type=F32)
         else:
-            total = gathered_sum(step)
             if step == 1:
                 for copy in rec_copies[1] + rec_passed:
                     copy.wait_recv()
+                current_of_field[...] = jnp.dot(
+                    rec_full[...], inv[...], preferred_element_type=F32
+                ).astype(BF16)
+                slab_of_field[...] = lax.dot_general(
+                    slab_of_drive[...], rec_full[...], dims, preferred_element_type=F32
+                ).astype(BF16)
+            known = gathered_sum(step).astype(BF16)
+            current = jnp.dot(known, inv[...], preferred_element_type=F32)
+            if more:
+                slab = lax.dot_general(slab_of_drive[...], known, dims, preferred_element_type=F32)
             wait_blocks(f_recv.at[step], f_sems.at[step, 1])
             field = turn_field([f_recv[step, k] for k in range(m * chunks)])
-            far = jnp.dot(field, rec_full[...], preferred_element_type=F32)
-            drive = (total - far).astype(BF16)
-        current = jnp.dot(drive, inv[...], preferred_element_type=F32).astype(BF16)
-        if step + 1 < steps:
-            slab = lax.dot_general(slab_of_drive[...], drive, dims, preferred_element_type=F32)
+            current = (
+                current - jnp.dot(field, current_of_field[...], preferred_element_type=F32)
+            ).astype(BF16)
+            if more:
+                slab = slab - lax.dot_general(
+                    slab_of_field[...], field, dims, preferred_element_type=F32
+                )
+        if more:
             wide = jnp.concatenate([slab[: rays // 2], slab[rays // 2 :]], axis=1)
         own[step] = current
         if step + 1 < steps:
@@ -584,6 +608,8 @@
                 vmem((size, size), BF16),
                 vmem((rays, size), BF16),
                 vmem((m * rays, size), BF16),
+                vmem((rays, m * rays), BF16),
+                vmem((m * rays, width), BF16),
                 vmem((spread, slots, waves, width), BF16),
                 vmem((spread, waves, width), BF16),
                 vmem((spread, waves, width), BF16),

time: 62.9 us -> 62.8 us (level)
  no operation moved by 1% of the time
where the time goes in v7:
time: 62.8 us; the launch traced here: 62.7 us
  Pallas kernels  61.4 us (98%)
  between operations  0.66 us (1%)
    pallas_call x1, Pallas kernels, local(): pl.pallas_call(functools.partial(kernel, n, inner, copies_of_fold, m), ou...  61.4 us

profile of v7, /device:TPU:1, one launch (start us, length us, event | category | flops | bytes accessed | tf_op | source)
XLA Modules:
  0.0 62.7 jit_solution(9472783355652118282)
XLA Ops:
  0.7 61.4 %shard_map.100 = bf16[3,64,128]{2,1,0:T(8,128)(2,1)S(1)} custom-call(bf16[3,64,128]{2,1,0:T(8,128)(2,1)} %exc_hbm.1, bf16[8,64,128]{2,1,0:T(8,128)(2,1)} %cyc_hbm.1, bf16[1,5,8,128,512]{4,3,2,1,0:T(8,128)(2,1)} %blocks_hbm.1, s32[1,5]{1,0:T(1,128)} %list_hbm.1, s32[1]{0:T(128)S(6)} %copy.13.count_hbm, s32[8]{0:T(128)} %newest_hbm.1, ...), custom_call_target="tpu_custom_call" | custom-call | tf_op jit(solution)/shard_map/pallas_call | solution.py:590
  62.1 0.6 copy.12

commit v8 on v7

--- a/solution.py
+++ b/solution.py
@@ -311,7 +311,25 @@
         ),
     ]
     rec_passed = ring_copies(rec_part, 6) if m == 4 else []
-    p_copies = []
+
+    def waves_of(k):
+        return pl.ds(k * (waves // 2), waves // 2)
+
+    def first_part(d, k):
+        part = p_recv.at[0, other_ray(m - d), waves_of(k), :]
+        return part, part
+
+    first_copies = [
+        ring_copies(
+            lambda d, k: (p_send.at[0, waves_of(k), :], p_recv.at[0, r, waves_of(k), :]), 7
+        ),
+        ring_copies(
+            lambda d, k: (p_send.at[0, waves_of(1 - k), :], p_recv.at[0, r, waves_of(1 - k), :]),
+            8,
+        ),
+    ]
+    first_passed = ring_copies(first_part, 9) if m == 4 else []
+    p_copies = [first_copies[1] + first_passed]
 
     def send_slab(step, wide):
         for k in range(chunks):
@@ -467,8 +485,14 @@
             wait_blocks(f_recv.at[0], f_sems.at[0, 1], chunks - 1)
             field = turn_field([f_recv[0, r * chunks + k] for k in range(chunks)])
             far = jnp.dot(field, rec_full[rows_here, :], preferred_element_type=F32)
-            send_partial(0, (base[0] - far).astype(BF16))
-            for copy in rec_copies[0]:
+            term = (base[0] - far).astype(BF16)
+            p_send[0] = term
+            for copy in first_copies[0] + first_copies[1]:
+                copy.start()
+            p_recv[0, r] = term
+            for copy in first_copies[0]:
+                copy.wait_recv()
+            for copy in first_passed + rec_copies[0]:
                 copy.start()
             load_rad.wait()
             load_inv.wait()
@@ -542,7 +566,7 @@
             for later in range(step + 2, steps):
                 add_near(later)
 
-    ringed = inv_copies + inv_passed + sum(rec_copies, rec_passed)
+    ringed = inv_copies + inv_passed + sum(rec_copies, rec_passed) + first_copies[0]
     for copy in slab_copies + rad_copies + ringed + near_all + sum(p_copies, []):
         copy.wait_send()
     wait_blocks(w_send, w_sems.at[0])
@@ -628,8 +652,8 @@
                 vmem((steps, waves, width), BF16),
                 pltpu.SemaphoreType.REGULAR,
                 dma((13,)),
-                dma((7, m - 1)),
-                dma((7, m - 1)),
+                dma((10, m - 1)),
+                dma((10, m - 1)),
                 dma((2,)),
                 dma((steps, 2)),
                 dma((steps, 2)),

time: 62.8 us -> 63.4 us (level)
  no operation moved by 1% of the time
where the time goes in v8:
time: 63.4 us; the launch traced here: 63.3 us
  Pallas kernels  62 us (98%)
  between operations  0.66 us (1%)
    pallas_call x1, Pallas kernels, local(): pl.pallas_call(functools.partial(kernel, n, inner, copies_of_fold, m), ou...  62 us

profile of v8, /device:TPU:1, one launch (start us, length us, event | category | flops | bytes accessed | tf_op | source)
XLA Modules:
  0.0 63.3 jit_solution(5305342237328509197)
XLA Ops:
  0.7 62.0 %shard_map.100 = bf16[3,64,128]{2,1,0:T(8,128)(2,1)S(1)} custom-call(bf16[3,64,128]{2,1,0:T(8,128)(2,1)} %exc_hbm.1, bf16[8,64,128]{2,1,0:T(8,128)(2,1)} %cyc_hbm.1, bf16[1,5,8,128,512]{4,3,2,1,0:T(8,128)(2,1)} %blocks_hbm.1, s32[1,5]{1,0:T(1,128)} %list_hbm.1, s32[1]{0:T(128)S(6)} %copy.13.count_hbm, s32[8]{0:T(128)} %newest_hbm.1, ...), custom_call_target="tpu_custom_call" | custom-call | tf_op jit(solution)/shard_map/pallas_call | solution.py:614
  62.6 0.6 copy.12

commit v9 on v7

--- a/solution.py
+++ b/solution.py
@@ -235,6 +235,8 @@
             rs_send[ray] = block
             copy.start()
     cycle_copies = near_copies(cyc_hbm, nearby, 0)
+    for copy in cycle_copies:
+        copy.start()
     near_all = list(cycle_copies)
 
     load_list.wait()
@@ -392,19 +394,7 @@
     for k in range(1, m):
         first_slab = first_slab + rs_recv[k].astype(F32)
     send_slab(0, first_slab)
-    for copy in cycle_copies + inv_copies + rad_copies:
-        copy.start()
-
-    wait_blocks(w_recv, w_sems.at[1])
-    for i in range(rows):
-        w_all = w_recv[:, i, :]
-        w_high = w_all.astype(BF16)
-        w_both[i, :chunks] = w_high
-        w_both[i, chunks:] = (w_all - w_high.astype(F32)).astype(BF16)
-    fold(0)
     for copy in inv_copies:
-        copy.wait_recv()
-    for copy in inv_passed:
         copy.start()
 
     load_self.wait()
@@ -439,6 +429,18 @@
 
 
     lax.fori_loop(0, entries, add_cycle, 0)
+
+    wait_blocks(w_recv, w_sems.at[1])
+    for i in range(rows):
+        w_all = w_recv[:, i, :]
+        w_high = w_all.astype(BF16)
+        w_both[i, :chunks] = w_high
+        w_both[i, chunks:] = (w_all - w_high.astype(F32)).astype(BF16)
+    fold(0)
+    for copy in inv_copies:
+        copy.wait_recv()
+    for copy in inv_passed + rad_copies:
+        copy.start()
 
     def gathered_sum(step):
         for copy in p_copies[step]:

time: 62.8 us -> 64.9 us (1.033)
  Pallas kernels: 61.4 us -> 63.6 us
    pallas_call x1, Pallas kernels: 61.4 us -> 63.6 us  [local(): pl.pallas_call(functools.partial(kernel, n, inner, copies_of_fold, m), ou...]
where the time goes in v9:
time: 64.9 us
  Pallas kernels  63.6 us (98%)
  between operations  0.66 us (1%)
    pallas_call x1, Pallas kernels, local(): pl.pallas_call(functools.partial(kernel, n, inner, copies_of_fold, m), ou...  63.6 us

profile of v9, /device:TPU:1, one launch (start us, length us, event | category | flops | bytes accessed | tf_op | source)
XLA Modules:
  0.0 64.9 jit_solution(9394438152818331981)
XLA Ops:
  0.7 63.6 %shard_map.100 = bf16[3,64,128]{2,1,0:T(8,128)(2,1)S(1)} custom-call(bf16[3,64,128]{2,1,0:T(8,128)(2,1)} %exc_hbm.1, bf16[8,64,128]{2,1,0:T(8,128)(2,1)} %cyc_hbm.1, bf16[1,5,8,128,512]{4,3,2,1,0:T(8,128)(2,1)} %blocks_hbm.1, s32[1,5]{1,0:T(1,128)} %list_hbm.1, s32[1]{0:T(128)S(6)} %copy.13.count_hbm, s32[8]{0:T(128)} %newest_hbm.1, ...), custom_call_target="tpu_custom_call" | custom-call | tf_op jit(solution)/shard_map/pallas_call | solution.py:592
  64.2 0.6 copy.12

commit v10 on v7

--- a/solution.py
+++ b/solution.py
@@ -402,10 +402,6 @@
         w_both[i, :chunks] = w_high
         w_both[i, chunks:] = (w_all - w_high.astype(F32)).astype(BF16)
     fold(0)
-    for copy in inv_copies:
-        copy.wait_recv()
-    for copy in inv_passed:
-        copy.start()
 
     load_self.wait()
     load_blocks.wait()
@@ -416,29 +412,43 @@
     for step in range(steps):
         base[step, :, mine] = exc[step].astype(F32)
 
-    def add_cycle(b, carry):
+    def add_cycle(b, first, last):
         shift = list_ref[0, b]
         source = g + shift - REACH
         valid = (b < count_ref[0]) & (source >= 0) & (source < n)
-        past = [nearby[shift, lax.rem(start_slot - i + slots, slots)] for i in range(slots)]
+        past = [
+            nearby[shift, lax.rem(start_slot - i + slots, slots)] for i in range(slots - first)
+        ]
         past = [jnp.where(valid, x, jnp.zeros_like(x)) for x in past]
         blank = jnp.zeros_like(past[0])
         lagged = jnp.concatenate(
             [
-                jnp.concatenate([blank] * step + past[: slots - step], axis=1)
-                for step in range(steps)
+                jnp.concatenate([blank] * k + past[: len(past) - k], axis=1)
+                for k in range(last - first)
             ],
             axis=0,
         )
         near = jnp.dot(
-            lagged, blocks[b].reshape(slots * width, size), preferred_element_type=F32
+            lagged,
+            blocks[b, first:].reshape((slots - first) * width, size),
+            preferred_element_type=F32,
         )
-        for step in range(steps):
-            base[step] = base[step] - near[step * waves : (step + 1) * waves]
+        for k in range(last - first):
+            base[first + k] = base[first + k] - near[k * waves : (k + 1) * waves]
+
+    def add_first(b, carry):
+        add_cycle(b, 0, 1)
         return carry
 
-
-    lax.fori_loop(0, entries, add_cycle, 0)
+    def add_later(b, carry):
+        add_cycle(b, 1, steps)
+        return carry
+
+    lax.fori_loop(0, entries, add_first, 0)
+    for copy in inv_copies:
+        copy.wait_recv()
+    for copy in inv_passed:
+        copy.start()
 
     def gathered_sum(step):
         for copy in p_copies[step]:
@@ -478,6 +488,7 @@
             slab_of_drive[...] = lax.dot_general(
                 rad_full[...], inv_full[...], dims, preferred_element_type=F32
             ).astype(BF16)
+            lax.fori_loop(0, entries, add_later, 0)
             drive = gathered_sum(0).astype(BF16)
             current = jnp.dot(drive, inv[...], preferred_element_type=F32).astype(BF16)
             slab = lax.dot_general(slab_of_drive[...], drive, dims, preferred_element_type=F32)

time: 62.8 us -> 63.5 us (1.011)
  Pallas kernels: 61.4 us -> 62.2 us
    pallas_call x1, Pallas kernels: 61.4 us -> 62.2 us  [local(): pl.pallas_call(functools.partial(kernel, n, inner, copies_of_fold, m), ou...]
where the time goes in v10:
time: 63.5 us; the launch traced here: 63.4 us
  Pallas kernels  62.2 us (98%)
  between operations  0.66 us (1%)
    pallas_call x1, Pallas kernels, local(): pl.pallas_call(functools.partial(kernel, n, inner, copies_of_fold, m), ou...  62.2 us

profile of v10, /device:TPU:1, one launch (start us, length us, event | category | flops | bytes accessed | tf_op | source)
XLA Modules:
  0.0 63.4 jit_solution(11401411086642953915)
XLA Ops:
  0.7 62.2 %shard_map.100 = bf16[3,64,128]{2,1,0:T(8,128)(2,1)S(1)} custom-call(bf16[3,64,128]{2,1,0:T(8,128)(2,1)} %exc_hbm.1, bf16[8,64,128]{2,1,0:T(8,128)(2,1)} %cyc_hbm.1, bf16[1,5,8,128,512]{4,3,2,1,0:T(8,128)(2,1)} %blocks_hbm.1, s32[1,5]{1,0:T(1,128)} %list_hbm.1, s32[1]{0:T(128)S(6)} %copy.13.count_hbm, s32[8]{0:T(128)} %newest_hbm.1, ...), custom_call_target="tpu_custom_call" | custom-call | tf_op jit(solution)/shard_map/pallas_call | solution.py:601
  62.8 0.6 copy.12

commit v11 on v7

--- a/solution.py
+++ b/solution.py
@@ -214,26 +214,28 @@
         load_exc,
     ) = loads
 
-    pl.semaphore_wait(barrier, len(greeted))
-
-    for device in row_peers:
-        pl.semaphore_signal(row_sem, inc=1, device_id=device, device_id_type=MESH)
     load_newest.wait()
     load_cyc.wait()
     start_slot = newest_ref[0]
     newest_value = cyc[start_slot]
     load_all_rad.wait()
-    slab_copies = ray_copies(lambda d: rs_send.at[other_ray(d)], rs_recv.at[r], 0)
-    for d, copy in zip(ray_order + [0], slab_copies + [None]):
+    for d in ray_order + [0]:
         ray = other_ray(d)
         block = rad[pl.ds(pl.multiple_of(ray * rays, rays), rays), :]
         block = lax.dot_general(block, newest_value, dims, preferred_element_type=F32)
         block = jnp.concatenate([block[: rays // 2], block[rays // 2 :]], axis=1).astype(BF16)
-        if copy is None:
+        if d:
+            rs_send[ray] = block
+        else:
             rs_recv[r] = block
-        else:
-            rs_send[ray] = block
-            copy.start()
+
+    pl.semaphore_wait(barrier, len(greeted))
+
+    slab_copies = ray_copies(lambda d: rs_send.at[other_ray(d)], rs_recv.at[r], 0)
+    for copy in slab_copies:
+        copy.start()
+    for device in row_peers:
+        pl.semaphore_signal(row_sem, inc=1, device_id=device, device_id_type=MESH)
     cycle_copies = near_copies(cyc_hbm, nearby, 0)
     near_all = list(cycle_copies)
 

time: 62.8 us -> 62.8 us (level)
  no operation moved by 1% of the time
where the time goes in v11:
time: 62.8 us
  Pallas kernels  61.5 us (98%)
  between operations  0.66 us (1%)
    pallas_call x1, Pallas kernels, local(): pl.pallas_call(functools.partial(kernel, n, inner, copies_of_fold, m), ou...  61.5 us

profile of v11, /device:TPU:1, one launch (start us, length us, event | category | flops | bytes accessed | tf_op | source)
XLA Modules:
  0.0 62.8 jit_solution(5843812461447421043)
XLA Ops:
  0.7 61.5 %shard_map.100 = bf16[3,64,128]{2,1,0:T(8,128)(2,1)S(1)} custom-call(bf16[3,64,128]{2,1,0:T(8,128)(2,1)} %exc_hbm.1, bf16[8,64,128]{2,1,0:T(8,128)(2,1)} %cyc_hbm.1, bf16[1,5,8,128,512]{4,3,2,1,0:T(8,128)(2,1)} %blocks_hbm.1, s32[1,5]{1,0:T(1,128)} %list_hbm.1, s32[1]{0:T(128)S(6)} %copy.13.count_hbm, s32[8]{0:T(128)} %newest_hbm.1, ...), custom_call_target="tpu_custom_call" | custom-call | tf_op jit(solution)/shard_map/pallas_call | solution.py:592
  62.1 0.6 copy.12
